TPU v7x, 32 devices: a whole 2x2x4 slice. The times are simulated.
32 devices in a mesh: ctx: 32 (over z, y, x, core), head: 1.
Axes of the slice: x: 2, y: 2, z: 4, core: 2. Of those that a mesh axis runs over, the one named last changes fastest.
Arguments:
- queries: bfloat16 [256, 4096], P('head', 'ctx'), may hold values from -6 to 6
- keys: bfloat16 [256, 4096], P('head', 'ctx'), may hold values from -6 to 6
- values: bfloat16 [4096, 2048], P('ctx', 'head'), may hold values from -6 to 6
- seg_ids: int32 [4096], P('ctx'), may hold values from 0 to 3, never falling along the last dimension, each value on 1 to 2048 neighbouring positions
- conv_weight: bfloat16 [3, 256], P(None, 'head'), may hold values from -3.5 to 3.5
- out_weight: bfloat16 [2048, 4096], P('head'), may hold values from -0.125 to 0.125
- out_grad: bfloat16 [4096, 4096], P('ctx', 'head'), may hold values from -6 to 6
Outputs:
- grad_queries: float32 [256, 4096], P('head', 'ctx')
- grad_keys: float32 [256, 4096], P('head', 'ctx')
- grad_values: float32 [4096, 2048], P('ctx', 'head')
Inputs may be any that keep to these rules, and one draw needn't show every extreme that they name: `seg_ids`: document numbers never fall along the sequence; each document holds 1 to 2048 tokens, and one holds exactly 2048.
All inputs are finite; a program needn't handle non-finite values.
Results may differ from a plain program's by a relative error of at most 0.0005.
Values may be sent and summed in bfloat16 or wider, within the bound.
A program may use at most 128 MiB of HBM per device.

v0:
```python
import jax
import jax.numpy as jnp
import numpy as np
from jax import lax
from jax.sharding import PartitionSpec as P

FD = 16


half_root = 0.7071067811865476
split_mode = lax.Precision.HIGH


def entering(shard, axis, combine, identity, reverse):
    size, here = (lax.axis_size(axis), lax.axis_index(axis))
    everything = jax.tree.map(lambda part: lax.all_gather(part, axis), shard)
    start = jax.tree.map(
        lambda part, zero: jnp.broadcast_to(jnp.asarray(zero, part.dtype), part.shape),
        shard,
        identity,
    )

    def step(k, before):
        at = size - 1 - k if reverse else k
        reached = at > here if reverse else at < here
        new = combine(before, jax.tree.map(lambda part: part[at], everything))
        return jax.tree.map(lambda a, b: jnp.where(reached, a, b), new, before)

    return lax.fori_loop(0, size, step, start)


def features(entries):
    scaled = entries * 0.5
    row_index, col_index = np.triu_indices(scaled.shape[-2], 1)
    cross = jnp.take(scaled, row_index, axis=-2) * jnp.take(scaled, col_index, axis=-2)
    return jnp.concatenate(
        [jnp.ones_like(scaled[..., :1, :]), scaled, scaled * scaled * half_root, cross], axis=-2
    )


def block_output(q_feat, k_feat, head_values, doc_ids, carry_mask, state_in, normer_in):
    length = doc_ids.shape[0]
    causal = jnp.arange(length)[:, None] >= jnp.arange(length)[None, :]
    allowed = (causal & (doc_ids[:, None] == doc_ids[None, :])).astype(jnp.float32)
    scores = jnp.einsum("hft,hfs->hts", q_feat, k_feat, precision=split_mode) * allowed[None, :, :]
    numerator = jnp.einsum("hts,shd->thd", scores, head_values, precision=split_mode)
    numerator = numerator + carry_mask[:, None, None] * jnp.einsum(
        "hft,hfd->thd", q_feat, state_in, precision=split_mode
    )
    denominator = jnp.sum(scores, axis=2).T + carry_mask[:, None] * jnp.einsum(
        "hft,hf->th", q_feat, normer_in, precision=split_mode
    )
    return numerator / denominator[:, :, None]


def join_forward(earlier, later):
    empty_later = later[0][1] == 0.0
    same_doc = earlier[0][1] == later[0][1]
    state_out = jnp.where(empty_later, earlier[2], later[2] + jnp.where(same_doc, earlier[2], 0.0))
    normer_out = jnp.where(empty_later, earlier[3], later[3] + jnp.where(same_doc, earlier[3], 0.0))
    return (
        jnp.where(empty_later, earlier[0], later[0]),
        jnp.where(empty_later, earlier[1], later[1]),
        state_out,
        normer_out,
    )


def join_backward(earlier, later):
    empty_later = later[0][0] == 0.0
    same_doc = earlier[0][0] == later[0][0]
    state_out = jnp.where(empty_later, earlier[2], later[2] + jnp.where(same_doc, earlier[2], 0.0))
    normer_out = jnp.where(empty_later, earlier[3], later[3] + jnp.where(same_doc, earlier[3], 0.0))
    return (
        jnp.where(empty_later, earlier[0], later[0]),
        jnp.where(empty_later, earlier[1], later[1]),
        state_out,
        normer_out,
    )


def body(queries, keys, values, seg_ids, conv_weight, out_weight, out_grad):
    local_heads = queries.shape[0] // FD
    length = queries.shape[1]
    head_width = values.shape[1] // local_heads
    grad_attn = lax.dot_general(
        lax.all_gather(out_grad, "head", axis=1, tiled=True),
        out_weight,
        (((1,), (1,)), ((), ())),
        preferred_element_type=jnp.float32,
    )
    doc_ids = (seg_ids + 1).astype(jnp.float32)
    query_rows = queries.astype(jnp.float32)
    key_heads = keys.astype(jnp.float32).reshape(local_heads, FD, length)
    head_values = values.astype(jnp.float32).reshape(length, local_heads, head_width)
    taps = conv_weight.astype(jnp.float32)
    k_feat, feature_pullback = jax.vjp(features, key_heads)
    tail_mask = (doc_ids == doc_ids[length - 1]).astype(jnp.float32)
    tail_feat = k_feat * tail_mask[None, None, :]
    tail_state = jnp.einsum("hfs,shd->hfd", tail_feat, head_values, precision=split_mode)
    tail_normer = jnp.sum(tail_feat, axis=2)
    forward_piece = (doc_ids[length - 2 :], query_rows[:, length - 2 :], tail_state, tail_normer)
    before = entering(
        forward_piece, "ctx", join_forward, jax.tree.map(jnp.zeros_like, forward_piece), False
    )
    query_ext = jnp.concatenate([before[1], query_rows], axis=1)
    ids_before = jnp.concatenate([before[0], doc_ids])
    q_conv = taps[0][:, None] * query_rows
    for offset in (1, 2):
        same_doc = (ids_before[2 - offset : 2 - offset + length] == doc_ids).astype(jnp.float32)
        q_conv = (
            q_conv
            + taps[offset][:, None]
            * query_ext[:, 2 - offset : 2 - offset + length]
            * same_doc[None, :]
        )
    carry_mask = (doc_ids == before[0][1]).astype(jnp.float32)

    def local_forward(q_conv_in, k_feat_in, values_in, state_in, normer_in):
        q_feat = features(q_conv_in.reshape(local_heads, FD, length))
        result = block_output(
            q_feat, k_feat_in, values_in, doc_ids, carry_mask, state_in, normer_in
        )
        return result.reshape(length, local_heads * head_width)

    _, local_pullback = jax.vjp(local_forward, q_conv, k_feat, head_values, before[2], before[3])
    grad_qconv, grad_kfeat, grad_heads, grad_state, grad_normer = local_pullback(grad_attn)
    backward_piece = (doc_ids[:2], grad_qconv[:, :2], grad_state, grad_normer)
    after = entering(
        backward_piece, "ctx", join_backward, jax.tree.map(jnp.zeros_like, backward_piece), True
    )
    head_mask = (doc_ids == after[0][0]).astype(jnp.float32)
    flowing = (
        jnp.einsum("hfd,shd->hfs", after[2], head_values, precision=split_mode)
        + after[3][:, :, None]
    )
    grad_kfeat = grad_kfeat + flowing * head_mask[None, None, :]
    grad_heads = grad_heads + jnp.einsum(
        "hfs,hfd->shd", k_feat * head_mask[None, None, :], after[2], precision=split_mode
    )
    (grad_key_heads,) = feature_pullback(grad_kfeat)
    grad_ext = jnp.concatenate([grad_qconv, after[1]], axis=1)
    ids_after = jnp.concatenate([doc_ids, after[0]])
    grad_queries = taps[0][:, None] * grad_qconv
    for offset in (1, 2):
        same_doc = (ids_after[offset : offset + length] == doc_ids).astype(jnp.float32)
        grad_queries = (
            grad_queries
            + taps[offset][:, None] * grad_ext[:, offset : offset + length] * same_doc[None, :]
        )
    grad_keys = grad_key_heads.reshape(local_heads * FD, length)
    grad_values = grad_heads.reshape(length, local_heads * head_width)
    return (grad_queries, grad_keys, grad_values)


def solution(mesh):
    in_specs = (
        P("head", "ctx"),
        P("head", "ctx"),
        P("ctx", "head"),
        P("ctx"),
        P(None, "head"),
        P("head", None),
        P("ctx", "head"),
    )
    out_specs = (P("head", "ctx"), P("head", "ctx"), P("ctx", "head"))
    return jax.shard_map(body, mesh=mesh, in_specs=in_specs, out_specs=out_specs, check_vma=False)
```

profile of v0, /device:TPU:0, one launch (start us, length us, event | category | flops | bytes accessed | tf_op | source)
XLA Modules:
  0.0 1178.7 jit_solution(14730475100487742021)
XLA Ops:
  8.2 1.6 multiply_multiply_fusion.1
  14.4 1.7 gather_fusion
  16.1 1.8 bitcast_multiply_fusion.3
  18.7 1.8 copy.75
  22.3 43.1 %all-reduce.2 = (f32[64]{0:T(128)S(1)}, f32[64]{0:T(128)}) all-reduce(f32[64]{0:T(128)S(1)} %slice_dynamic-update-slice_fusion.1, f32[64]{0:T(128)S(1)} %slice_dynamic-update-slice_fusion), channel_id=2, replica_groups=mesh['ctx'=32,'head'=1] {'ctx'}, use_global_device_ids=true, to_apply=%add | all-reduce | flops 128 | bytes 1024
  66.1 91.3 %all-gather.1 = f32[8192,2]{1,0:T(8,128)} all-gather(f32[256,2]{1,0:T(8,128)S(1)} %slice.126), channel_id=3, replica_groups=mesh['ctx'=32,'head'=1] {'ctx'}, dimensions={0}, use_global_device_ids=true | all-gather | bytes 67584 | tf_op jit(solution)/shard_map/all_gather | solution.py:16
  157.4 4.8 copy.76
  162.2 1.6 multiply_reduce_fusion
  163.8 45.1 %all-gather.3 = f32[512,153]{1,0:T(8,128)} all-gather(f32[16,153]{1,0:T(8,128)S(1)} %multiply_reduce_fusion), channel_id=5, replica_groups=mesh['ctx'=32,'head'=1] {'ctx'}, dimensions={0}, use_global_device_ids=true | all-gather | bytes 323136 | tf_op jit(solution)/shard_map/all_gather | solution.py:16
  210.3 9.2 fusion.59
  219.5 82.3 %all-gather.11.cloned.1.call-done = f32[512,153,128]{2,0,1:T(8,128)} async-done(((f32[16,153,128]{2,0,1:T(8,128)}), f32[512,153,128]{2,0,1:T(8,128)}) %all-gather.11.cloned.1.call-update) | async-done | bytes 40108048 | tf_op jit(solution)/shard_map/all_gather | solution.py:16
  301.8 297.8 %while.42 = (s32[]{:T(128)}, f32[2]{0:T(128)}, f32[256,2]{0,1:T(2,128)S(1)}, f32[16,153,128]{2,1,0:T(8,128)S(1)}, f32[16,153]{1,0:T(8,128)}, /*index=5*/s32[]{:T...) while((s32[]{:T(128)}, f32[2]{0:T(128)}, ...), condition=%wide.region_2.4_spmd.clone, body=%wide.region_1.3_spmd.clone.sunk | while | flops 1580508 | bytes 6381059 | solution.py:29
  605.3 1.8 gather_fusion.2
  607.2 1.9 bitcast_multiply_fusion
  609.1 3.0 fusion.58
  614.6 1.8 copy.95
  617.2 3.6 fusion.6
  628.4 5.3 scatter_fusion
  633.8 10.7 scatter_fusion.1
  644.6 88.4 %all-gather.5 = f32[8192,2]{1,0:T(8,128)} all-gather(f32[256,2]{1,0:T(8,128)S(1)} %bitcast.220), channel_id=7, replica_groups=mesh['ctx'=32,'head'=1] {'ctx'}, dimensions={0}, use_global_device_ids=true | all-gather | bytes 67584 | tf_op jit(solution)/shard_map/all_gather | solution.py:16
  733.0 3.5 copy.96
  737.8 43.1 %all-gather.7 = f32[512,153]{1,0:T(8,128)} all-gather(f32[16,153]{1,0:T(8,128)S(1)} %bitcast.228), channel_id=9, replica_groups=mesh['ctx'=32,'head'=1] {'ctx'}, dimensions={0}, use_global_device_ids=true | all-gather | bytes 323136 | tf_op jit(solution)/shard_map/all_gather | solution.py:16
  780.9 108.4 %all-gather.13.cloned.1.call-done = f32[512,153,128]{2,0,1:T(8,128)} async-done(((f32[16,153,128]{2,0,1:T(8,128)}), f32[512,153,128]{2,0,1:T(8,128)}) %all-gather.13.cloned.1.call-update) | async-done | bytes 40108048 | tf_op jit(solution)/shard_map/all_gather | solution.py:16
  889.2 243.4 %while.43 = (s32[]{:T(128)}, f32[2]{0:T(128)}, f32[256,2]{0,1:T(2,128)S(1)}, f32[16,153,128]{2,1,0:T(8,128)S(1)}, f32[16,153]{1,0:T(8,128)}, /*index=5*/s32[]{:T...) while((s32[]{:T(128)}, f32[2]{0:T(128)}, ...), condition=%wide.region_8.10_spmd.clone, body=%wide.region_7.9_spmd.clone.sunk | while | flops 1580512 | bytes 6381165 | solution.py:29
  891.9 1.4 constant_dynamic-slice_fusion.11
  899.5 1.4 constant_dynamic-slice_fusion.11
  907.1 1.4 constant_dynamic-slice_fusion.11
  914.8 1.4 constant_dynamic-slice_fusion.11
  922.4 1.4 constant_dynamic-slice_fusion.11
  929.9 1.4 constant_dynamic-slice_fusion.11
  937.6 1.4 constant_dynamic-slice_fusion.11
  945.1 1.4 constant_dynamic-slice_fusion.11
  952.6 1.4 constant_dynamic-slice_fusion.11
  960.2 1.4 constant_dynamic-slice_fusion.11
  967.8 1.4 constant_dynamic-slice_fusion.11
  975.4 1.4 constant_dynamic-slice_fusion.11
  983.0 1.4 constant_dynamic-slice_fusion.11
  990.6 1.4 constant_dynamic-slice_fusion.11
  998.2 1.4 constant_dynamic-slice_fusion.11
  1005.7 1.4 constant_dynamic-slice_fusion.11
  1013.4 1.4 constant_dynamic-slice_fusion.11
  1021.0 1.4 constant_dynamic-slice_fusion.11
  1028.7 1.4 constant_dynamic-slice_fusion.11
  1036.3 1.4 constant_dynamic-slice_fusion.11
  1043.9 1.4 constant_dynamic-slice_fusion.11
  1051.5 1.4 constant_dynamic-slice_fusion.11
  1059.2 1.4 constant_dynamic-slice_fusion.11
  1066.8 1.4 constant_dynamic-slice_fusion.11
  1074.4 1.4 constant_dynamic-slice_fusion.11
  1082.0 1.4 constant_dynamic-slice_fusion.11
  1089.6 1.4 constant_dynamic-slice_fusion.11
  1097.2 1.4 constant_dynamic-slice_fusion.11
  1104.8 1.4 constant_dynamic-slice_fusion.11
  1112.5 1.4 constant_dynamic-slice_fusion.11
  1120.1 1.4 constant_dynamic-slice_fusion.11
  1127.8 1.4 constant_dynamic-slice_fusion.11
  1133.4 1.9 compare_convert_fusion.2
  1135.3 2.1 fusion.2
  1139.4 1.6 fusion.21
  1141.1 3.0 fusion.7
  1147.7 5.3 scatter_fusion.2
  1153.1 10.8 scatter_fusion.3
  1164.7 3.6 convolution_add_fusion.4
  1168.2 2.6 copy.106
  (938 shorter events, 426.7 us)
Async XLA Ops:
  7.2 203.1 %copy-start = (bf16[128,4096]{1,0:T(8,128)(2,1)S(1)}, bf16[128,4096]{1,0:T(8,128)(2,1)}, u32[]{:S(2)}) copy-start(bf16[128,4096]{1,0:T(8,128)(2,1)} %param.23) | copy-start | bytes 3145732
  7.2 294.6 %all-gather.11.cloned.1.call-start = ((), (), s32[]{:S(2)}) async-start(), calls=%async_computation | async-start | bytes 41361408 | tf_op jit(solution)/shard_map/all_gather | solution.py:16
  8.2 9.8 copy-start.19
  12.3 5.7 copy-start.65
  13.0 3.1 copy-start.58
  13.7 2.4 copy-start.59
  14.4 3.6 copy-start.6
  20.5 868.8 %all-gather.13.cloned.1.call-start = ((), (), s32[]{:S(2)}) async-start(), calls=%async_computation.1 | async-start | bytes 41361408 | tf_op jit(solution)/shard_map/all_gather | solution.py:16
  157.4 4.8 copy-start.20
  157.4 4.8 copy-start.66
  162.2 46.8 %copy-start.60 = (bf16[3,256]{1,0:T(4,128)(2,1)S(1)}, bf16[3,256]{1,0:T(4,128)(2,1)}, u32[]{:S(2)}) copy-start(bf16[3,256]{1,0:T(4,128)(2,1)} %param.21) | copy-start | bytes 4612
  599.6 9.5 copy-start.2
  603.0 9.8 copy-start.52
  604.4 132.2 %copy-start.17 = (f32[256,128]{1,0:T(8,128)}, f32[256,128]{1,0:T(8,128)S(1)}, u32[]{:S(2)}) copy-start(f32[256,128]{1,0:T(8,128)S(1)} %fusion.45) | copy-start | bytes 393220
  605.3 3.8 copy-start.9
  607.1 5.7 copy-start.32
  609.1 3.8 copy-start.12
  609.1 3.0 copy-start.43
  612.8 9.4 copy-start.47
  614.6 2.6 copy-start.53
  617.2 3.6 copy-start.16
  617.2 3.7 copy-start.24
  628.4 5.4 copy-start.61
  644.6 88.4 %copy-start.35 = (f32[16,16,128]{2,1,0:T(8,128)}, f32[16,16,128]{2,1,0:T(8,128)S(1)}, u32[]{:S(2)}) copy-start(f32[16,16,128]{2,1,0:T(8,128)S(1)} %copy.94) | copy-start | bytes 393220
  733.0 3.6 copy-start.13
  733.0 3.6 copy-start.33
  733.0 3.6 copy-start.57
  897.5 2.0 copy-start.70
  905.1 2.0 copy-start.70
  912.7 2.0 copy-start.70
  920.4 2.0 copy-start.70
  935.5 2.0 copy-start.70
  958.2 2.0 copy-start.70
  973.4 2.0 copy-start.70
  988.6 2.0 copy-start.70
  996.2 2.0 copy-start.70
  1011.3 2.0 copy-start.70
  1019.0 2.0 copy-start.70
  1026.6 2.0 copy-start.70
  1034.3 2.0 copy-start.70
  1041.9 2.0 copy-start.70
  1057.2 2.0 copy-start.70
  1072.4 2.0 copy-start.70
  1087.6 2.0 copy-start.70
  1110.4 2.0 copy-start.70
  1118.1 2.0 copy-start.70
  1125.7 2.0 copy-start.70
  1135.2 2.1 copy-start.14
  1135.2 2.1 copy-start.18
  1135.3 2.1 copy-start.27
  1135.3 2.1 copy-start.34
  1137.4 2.0 copy-start.7
  1137.4 2.0 copy-start.8
  1147.7 5.4 copy-start.62
  1153.1 11.6 copy-start.5
  1153.1 11.6 copy-start.25
  1153.1 11.5 copy-start.48
  1164.6 7.2 copy-start.1
  1168.2 2.6 copy-start.36
  1168.2 2.6 copy-start.49
  1168.2 2.6 copy-start.50
  1168.2 2.6 copy-start.51
  1168.2 2.6 copy-start.67
  1168.2 2.6 copy-start.68
  (164 other events, 152.9 us)
Sparse Core Ops, SparseCore 0:
  20.6 281.1 all-gather.10
  616.5 272.6 all-gather.12
where the time goes:
time: 1190 us; the launch traced here: 1180 us
  blocking collectives  311 us (26%)
  other arithmetic  279 us (23%)
  local copies, waits for them, and re-layouts  245 us (21%)
  waiting for transfers between devices  191 us (16%)
  loops' own time  106 us (9%)
  matrix products  32.6 us (3%)
  between operations  14.9 us (1%)
    all_gather x4, blocking collectives, entering(): everything = jax.tree.map(lambda part: lax.all_gather(part, axis), shard)  268 us
    select_n x256, other arithmetic, step(): return jax.tree.map(lambda a, b: jnp.where(reached, a, b), new, before)  224 us
    all_gather x2, waiting for transfers between devices, entering(): everything = jax.tree.map(lambda part: lax.all_gather(part, axis), shard)  191 us
    dynamic_slice x128, local copies, waits for them, and re-layouts, step(): new = combine(before, jax.tree.map(lambda part: part[at], everything))  133 us
    another operation x2, loops' own time, entering(): return lax.fori_loop(0, size, step, start)  106 us
    unnamed x1, blocking collectives  43.1 us
    while x320, local copies, waits for them, and re-layouts  38.7 us
  transfers between devices with their start and end apart: 2, of which 2 were waited for; matrix products, arithmetic and copies ran while one was open for 4% of the time, Pallas kernels for 0%

commit v1 on v0

--- a/solution.py
+++ b/solution.py
@@ -1,7 +1,8 @@
 import jax
 import jax.numpy as jnp
-import numpy as np
 from jax import lax
+from jax.experimental import pallas as pl
+from jax.experimental.pallas import tpu as pltpu
 from jax.sharding import PartitionSpec as P
 
 FD = 16
@@ -31,10 +32,11 @@
 
 def features(entries):
     scaled = entries * 0.5
-    row_index, col_index = np.triu_indices(scaled.shape[-2], 1)
-    cross = jnp.take(scaled, row_index, axis=-2) * jnp.take(scaled, col_index, axis=-2)
+    cross = [
+        scaled[..., i : i + 1, :] * scaled[..., i + 1 :, :] for i in range(scaled.shape[-2] - 1)
+    ]
     return jnp.concatenate(
-        [jnp.ones_like(scaled[..., :1, :]), scaled, scaled * scaled * half_root, cross], axis=-2
+        [jnp.ones_like(scaled[..., :1, :]), scaled, scaled * scaled * half_root] + cross, axis=-2
     )
 
 
@@ -153,6 +155,213 @@
     return (grad_queries, grad_keys, grad_values)
 
 
+f32, bf16 = jnp.float32, jnp.bfloat16
+NN = (((1,), (0,)), ((), ()))
+NT = (((1,), (1,)), ((), ()))
+TN = (((0,), (0,)), ((), ()))
+BLOCKS = 2
+SEG_ROW = 2 * FD
+V_ROW = 3 * FD
+
+
+def split(x):
+    high = x.astype(bf16)
+    return high, (x - high.astype(f32)).astype(bf16)
+
+
+def dot(a, b, dims):
+    return lax.dot_general(a, b, dims, preferred_element_type=f32)
+
+
+def dot3(a, b, dims):
+    return dot(a[0], b[0], dims) + dot(a[0], b[1], dims) + dot(a[1], b[0], dims)
+
+
+def ahead(x, d):
+    return pltpu.roll(x, FD - d, 0)
+
+
+def phi(u):
+    rows = [u, u * u * half_root]
+    for d in range(1, FD // 2):
+        rows.append(u * ahead(u, d))
+    half = FD // 2
+    one = (lax.broadcasted_iota(jnp.int32, (half, u.shape[1]), 0) == 0).astype(f32)
+    rows.append(jnp.concatenate([u[:half] * u[half:], one], axis=0))
+    return jnp.concatenate(rows, axis=0)
+
+
+def phi_pullback(u, grad):
+    total = grad[:FD] + (2.0 * half_root) * u * grad[FD : 2 * FD]
+    for d in range(1, FD // 2):
+        part = grad[(d + 1) * FD : (d + 2) * FD]
+        total = total + part * ahead(u, d) + pltpu.roll(part * u, d, 0)
+    half = FD // 2
+    last = grad[(half + 1) * FD : (half + 1) * FD + half]
+    return total + jnp.concatenate([last * u[half:], last * u[:half]], axis=0)
+
+
+def head_kernel(pk_ref, g_ref, meta_ref, taps_ref, out_ref, u_ref, du_ref, gext_ref):
+    blocks, width = pk_ref.shape[0], pk_ref.shape[2]
+    channels = g_ref.shape[1]
+    ext = channels + FD
+    seq = blocks * width
+    size = BLOCKS * width
+    chunks = blocks // BLOCKS
+    nf = (FD // 2 + 2) * FD
+
+    def load(ref, i, start, rows):
+        parts = [ref[i * BLOCKS + j, start : start + rows, :] for j in range(BLOCKS)]
+        return jnp.concatenate(parts, axis=1)
+
+    def store(i, start, x, add):
+        for j in range(BLOCKS):
+            part = x[:, j * width : (j + 1) * width]
+            rows = pl.ds(start, x.shape[0])
+            if add:
+                part = part + out_ref[i * BLOCKS + j, rows, :]
+            out_ref[i * BLOCKS + j, rows, :] = part
+
+    raw = jnp.concatenate([pk_ref[j, 0:FD, :].astype(f32) for j in range(blocks)], axis=1) * 0.5
+    u_ref[...] = (
+        taps_ref[:, 0:1] * raw
+        + taps_ref[:, 1:2] * pltpu.roll(raw, 1, 1) * meta_ref[4:5, :]
+        + taps_ref[:, 2:3] * pltpu.roll(raw, 2, 1) * meta_ref[5:6, :]
+    )
+    causal = lax.broadcasted_iota(jnp.int32, (size, size), 0) <= lax.broadcasted_iota(
+        jnp.int32, (size, size), 1
+    )
+    ones_rows = (lax.broadcasted_iota(jnp.int32, (FD, size), 0) == 0).astype(bf16)
+
+    def value_rows(i):
+        return jnp.concatenate([load(pk_ref, i, V_ROW, channels), ones_rows], axis=0)
+
+    def forward(i, state):
+        span = pl.ds(pl.multiple_of(i * size, size), size)
+        u = u_ref[:, span]
+        w16 = load(pk_ref, i, FD, FD) * jnp.asarray(0.5, bf16)
+        w = w16.astype(f32)
+        vext = value_rows(i)
+        g = load(g_ref, i, 0, channels)
+        seg = meta_ref[0:1, span]
+        carry = meta_ref[1:2, span]
+        tail = meta_ref[2:3, span]
+        keep = meta_ref[3:4, span][:, 0:1]
+        seg_t = jnp.broadcast_to(seg, (size, size))
+        allowed = jnp.where(causal & (seg_t == seg_t.T), 1.0, 0.0)
+        us = split(u)
+        x = dot(jnp.concatenate([w16, w16], axis=0), jnp.concatenate(us, axis=0), TN)
+        slope = allowed * (1.0 + x)
+        p = split(allowed * (1.0 + x + 0.5 * x * x))
+        feat_q = split(phi(u) * carry)
+        states = split(state)
+        numer = dot(vext, p[0], NN) + dot(vext, p[1], NN) + dot3(states, feat_q, NN)
+        inverse = 1.0 / numer[channels : channels + 1]
+        gp = g * inverse
+        dden = -jnp.sum(gp * numer[:channels], axis=0, keepdims=True) * inverse
+        gext = jnp.concatenate([gp, dden, jnp.zeros((FD - 1, size), f32)], axis=0)
+        gext_ref[:, span] = gext
+        gs = split(gext)
+        dx = split(slope * (dot(vext, gs[0], TN) + dot(vext, gs[1], TN)))
+        du = dot(w16, dx[0], NN) + dot(w16, dx[1], NN)
+        dw = dot3(us, dx, NT)
+        dv = dot3((gs[0][:channels], gs[1][:channels]), p, NT)
+        du_ref[:, span] = du + phi_pullback(u, dot3(states, gs, TN) * carry)
+        store(i, channels + FD, dw, False)
+        store(i, 0, dv, False)
+        feat_k = split(phi(w) * tail)
+        return keep * state + dot(vext, feat_k[0], NT) + dot(vext, feat_k[1], NT)
+
+    lax.fori_loop(0, chunks, forward, jnp.zeros((ext, nf), f32))
+
+    def backward(step, adjoint):
+        i = chunks - 1 - step
+        span = pl.ds(pl.multiple_of(i * size, size), size)
+        w = (load(pk_ref, i, FD, FD) * jnp.asarray(0.5, bf16)).astype(f32)
+        vext = value_rows(i)
+        tail = meta_ref[2:3, span]
+        keep = meta_ref[3:4, span][:, 0:1]
+        adj = split(adjoint)
+        feat_k = split(phi(w) * tail)
+        dfeat = (dot(adj[0], vext, TN) + dot(adj[1], vext, TN)) * tail
+        old = load(out_ref, i, channels + FD, FD)
+        store(i, channels + FD, 0.5 * (old + phi_pullback(w, dfeat)), False)
+        store(i, 0, dot3((adj[0][:channels], adj[1][:channels]), feat_k, NN), True)
+        feat_q = split(phi(u_ref[:, span]) * meta_ref[1:2, span])
+        return keep * adjoint + dot3(split(gext_ref[:, span]), feat_q, NT)
+
+    lax.fori_loop(0, chunks, backward, jnp.zeros((ext, nf), f32))
+    du = du_ref[...] * 0.5
+    dq = (
+        taps_ref[:, 0:1] * du
+        + taps_ref[:, 1:2] * pltpu.roll(du, seq - 1, 1) * meta_ref[6:7, :]
+        + taps_ref[:, 2:3] * pltpu.roll(du, seq - 2, 1) * meta_ref[7:8, :]
+    )
+    for j in range(blocks):
+        out_ref[j, channels : channels + FD, :] = dq[:, j * width : (j + 1) * width]
+
+
+def head_call(pk, g, meta, taps):
+    blocks, _, width = pk.shape
+    channels = g.shape[1]
+    return pl.pallas_call(
+        head_kernel,
+        out_shape=jax.ShapeDtypeStruct((blocks, channels + 2 * FD, width), f32),
+        in_specs=[pl.BlockSpec(memory_space=pltpu.VMEM)] * 4,
+        out_specs=pl.BlockSpec(memory_space=pltpu.VMEM),
+        scratch_shapes=[
+            pltpu.VMEM((FD, blocks * width), f32),
+            pltpu.VMEM((FD, blocks * width), f32),
+            pltpu.VMEM((channels + FD, blocks * width), f32),
+        ],
+        compiler_params=pltpu.CompilerParams(vmem_limit_bytes=40 * 2**20),
+    )(pk, g, meta, taps)
+
+
+def meta_rows(pk):
+    blocks, _, width = pk.shape
+    size = BLOCKS * width
+    seg = pk[:, SEG_ROW, :].astype(f32).reshape(-1)
+    last = jnp.repeat(seg[size - 1 :: size], size)
+    before = jnp.concatenate([jnp.full((size,), -1.0, f32), last[:-size]])
+    same = lambda a, b: (a == b).astype(f32)
+    late = lambda d: same(jnp.pad(seg, (d, 0), constant_values=-1.0)[:-d], seg)
+    soon = lambda d: same(jnp.pad(seg, (0, d), constant_values=-1.0)[d:], seg)
+    rows = [seg, same(seg, before), same(seg, last), same(before, last)]
+    return jnp.stack(rows + [late(1), late(2), soon(1), soon(2)])
+
+
+def pack(queries, keys, values, seg_ids, size):
+    heads, length = queries.shape[0] // FD, queries.shape[1]
+    share = size // heads
+    twice = lambda x: jnp.repeat(x.reshape(heads, FD, length), share, axis=0)
+    seg = jnp.broadcast_to(seg_ids.astype(bf16), (size, FD, length))
+    rows = values.T.reshape(size, -1, length)
+    return jnp.concatenate([twice(queries), twice(keys), seg, rows], axis=1)
+
+
+def by_heads(queries, keys, values, seg_ids, conv_weight, out_weight, out_grad):
+    size = lax.axis_size("ctx")
+    heads, length = queries.shape[0] // FD, queries.shape[1]
+    share = size // heads
+    swap = lambda x: lax.all_to_all(x, "ctx", 0, 0)
+    pk = swap(pack(queries, keys, values, seg_ids, size))
+    grad_attn = lax.dot_general(out_weight, out_grad, NT, preferred_element_type=f32)
+    g = swap(grad_attn.reshape(size, -1, length))
+    head = lax.axis_index("ctx") // share
+    taps = lax.dynamic_slice_in_dim(conv_weight.astype(f32).T, head * FD, FD, 0)
+    taps = jnp.pad(taps, ((0, 0), (0, 128 - taps.shape[1])))
+    out = swap(head_call(pk, g, meta_rows(pk), taps))
+    channels = g.shape[1]
+    joined = lambda x: x.reshape(heads, share, FD, length).sum(1).reshape(heads * FD, length)
+    grad_values = out[:, :channels].reshape(-1, length).T
+    return (
+        joined(out[:, channels : channels + FD]),
+        joined(out[:, channels + FD :]),
+        grad_values,
+    )
+
+
 def solution(mesh):
     in_specs = (
         P("head", "ctx"),
@@ -164,4 +373,13 @@
         P("ctx", "head"),
     )
     out_specs = (P("head", "ctx"), P("head", "ctx"), P("ctx", "head"))
-    return jax.shard_map(body, mesh=mesh, in_specs=in_specs, out_specs=out_specs, check_vma=False)
+
+    def program(queries, *rest):
+        heads = queries.shape[0] // FD
+        spread = mesh.shape["head"] == 1 and mesh.shape["ctx"] == 2 * heads
+        inner = by_heads if spread else body
+        return jax.shard_map(
+            inner, mesh=mesh, in_specs=in_specs, out_specs=out_specs, check_vma=False
+        )(queries, *rest)
+
+    return program

time: 1190 us -> 138 us (0.12)
  other arithmetic: 279 us -> 2.67 us
  blocking collectives: 311 us -> 41.4 us
  local copies, waits for them, and re-layouts: 245 us -> 7.22 us
  waiting for transfers between devices: 191 us -> 39.7 us
  loops' own time: 106 us -> 0 us
  Pallas kernels: 0 us -> 25.7 us
  matrix products: 32.6 us -> 9.1 us
  between operations: 14.9 us -> 0.76 us
    all_gather x4 -> x0, blocking collectives: 268 us -> none  [entering(): everything = jax.tree.map(lambda part: lax.all_gather(part, axis), shard)]
    select_n x256 -> x0, other arithmetic: 224 us -> none  [step(): return jax.tree.map(lambda a, b: jnp.where(reached, a, b), new, before)]
    all_gather x2 -> x0, waiting for transfers between devices: 191 us -> none  [entering(): everything = jax.tree.map(lambda part: lax.all_gather(part, axis), shard)]
    dynamic_slice x128 -> x0, local copies, waits for them, and re-layouts: 133 us -> none  [step(): new = combine(before, jax.tree.map(lambda part: part[at], everything))]
    another operation x2 -> x0, loops' own time: 106 us -> none  [entering(): return lax.fori_loop(0, size, step, start)]
    unnamed x1 -> x0, blocking collectives: 43.1 us -> none
    all_to_all x0 -> x1, blocking collectives: none -> 41.4 us  [by_heads(): swap = lambda x: lax.all_to_all(x, 'ctx', 0, 0)]
    slice x68 -> x3, local copies, waits for them, and re-layouts: 42.2 us -> 1.16 us  [the longest x1 1.06 us: by_heads(): grad_values = out[:, :channels].reshape(-1, length).T]
  transfers between devices with their start and end apart: 2 -> 2, of which waited for: 2 -> 2; matrix products, arithmetic and copies ran while one was open for 4% -> 7% of each run, Pallas kernels for 0% -> 0%
where the time goes in v1:
time: 138 us
  blocking collectives  41.4 us (30%)
  waiting for transfers between devices  39.7 us (29%)
  Pallas kernels  25.7 us (19%)
  starting transfers between devices  10.9 us (8%)
  matrix products  9.1 us (7%)
  local copies, waits for them, and re-layouts  7.22 us (5%)
  other arithmetic  2.67 us (2%)
    all_to_all x1, blocking collectives, by_heads(): swap = lambda x: lax.all_to_all(x, 'ctx', 0, 0)  41.4 us
    all_to_all x2, waiting for transfers between devices, by_heads(): swap = lambda x: lax.all_to_all(x, 'ctx', 0, 0)  39.7 us
    pallas_call x1, Pallas kernels, head_call(): pl.pallas_call(head_kernel, out_shape=jax.ShapeDtypeStruct((blocks, chann...  25.7 us
    all_to_all x2, starting transfers between devices, by_heads(): swap = lambda x: lax.all_to_all(x, 'ctx', 0, 0)  10.9 us
    dot_general x1, matrix products, by_heads(): lax.dot_general(out_weight, out_grad, NT, preferred_element_type=f32)  9.1 us
  transfers between devices with their start and end apart: 2, of which 2 were waited for; matrix products, arithmetic and copies ran while one was open for 7% of the time, Pallas kernels for 0%

profile of v1, /device:TPU:0, one launch (start us, length us, event | category | flops | bytes accessed | tf_op | source)
XLA Modules:
  0.0 137.5 jit_solution(15459567383633988958)
XLA Ops:
  0.6 0.0 copy-start
  0.6 0.7 convert_element_type.47
  1.4 1.3 copy.10
  2.7 0.9 broadcast_in_dim.15
  3.6 0.9 broadcast_in_dim.16
  4.5 1.0 pad_maximum_fusion
  5.5 7.3 %all-to-all-start = ((bf16[32,112,128]{2,1,0:T(8,128)(2,1)}), bf16[32,112,128]{2,1,0:T(8,128)(2,1)S(1)}, u32[]{:S(2)}, u32[]{:S(2)}) async-start(bf16[32,112,128]{2,1,0:T(8,128)(2,1)} %pad_maximum_fusion), calls=%async_computation | async-start | bytes 1835008 | tf_op jit(solution)/shard_map/all_to_all | solution.py:347
  12.8 0.0 copy-done
  12.8 9.1 %fusion.9 = f32[2048,128]{1,0:T(8,128)} fusion(bf16[2048,4096]{1,0:T(8,128)(2,1)} %param.12, bf16[128,4096]{1,0:T(8,128)(2,1)S(1)} %copy-done), kind=kOutput, calls=%fused_computation.23 | convolution fusion | flops 2147483648 | bytes 18874368 | tf_op jit(solution)/shard_map/dot_general | solution.py:349
  21.9 0.0 copy-start.1
  21.9 14.3 %all-to-all-done.pk_ref = bf16[32,112,128]{2,1,0:T(8,128)(2,1)S(1)} async-done(((bf16[32,112,128]{2,1,0:T(8,128)(2,1)}), bf16[32,112,128]{2,1,0:T(8,128)(2,1)S(1)}, u32[]{:S(2)}, u32[]{:S(2)}) %all-to-all-start) | async-done | bytes 917536 | tf_op jit(solution)/shard_map/all_to_all | solution.py:347
  36.2 3.6 %all-to-all-start.1 = ((f32[32,64,128]{2,1,0:T(8,128)}), f32[32,64,128]{2,1,0:T(8,128)S(1)}, u32[]{:S(2)}, u32[]{:S(2)}) async-start(f32[32,64,128]{2,1,0:T(8,128)} %bitcast.38), calls=%async_computation.1 | async-start | bytes 2097152 | tf_op jit(solution)/shard_map/all_to_all | solution.py:347
  39.8 0.0 copy-done.1
  39.8 0.1 dynamic-slice_convert_fusion
  39.9 0.1 copy.13
  40.0 0.1 slice.35
  40.1 0.1 broadcast_in_dim.18
  40.2 0.1 broadcast_bitcast_fusion
  40.3 0.1 fusion.4
  40.5 0.2 stack.52.meta_ref
  40.7 25.4 %all-to-all-done.1.g_ref = f32[32,64,128]{2,1,0:T(8,128)S(1)} async-done(((f32[32,64,128]{2,1,0:T(8,128)}), f32[32,64,128]{2,1,0:T(8,128)S(1)}, u32[]{:S(2)}, u32[]{:S(2)}) %all-to-all-start.1) | async-done | bytes 1048608 | tf_op jit(solution)/shard_map/all_to_all | solution.py:347
  66.1 25.7 %shard_map.94 = f32[32,96,128]{2,1,0:T(8,128)S(1)} custom-call(bf16[32,112,128]{2,1,0:T(8,128)(2,1)S(1)} %all-to-all-done.pk_ref, f32[32,64,128]{2,1,0:T(8,128)S(1)} %all-to-all-done.1.g_ref, f32[8,4096]{1,0:T(8,128)S(1)} %stack.52.meta_ref, f32[16,128]{1,0:T(8,128)S(1)} %pad.25.taps_ref), custom_call_target="tpu_custom_call" | custom-call | tf_op jit(solution)/shard_map/pallas_call | solution.py:307
  91.7 41.4 %all_to_all.15 = f32[32,96,128]{2,1,0:T(8,128)S(1)} all-to-all(f32[32,96,128]{2,1,0:T(8,128)S(1)} %shard_map.94), channel_id=1, replica_groups=mesh['ctx'=32,'head'=1] {'ctx'}, dimensions={0} | all-to-all | bytes 3145728 | tf_op jit(solution)/shard_map/all_to_all | solution.py:347
  133.2 1.1 slice.48
  134.2 2.5 %copy.12 = f32[2048,128]{0,1:T(8,128)} copy(f32[2048,128]{1,0:T(8,128)} %bitcast.36) | data formatting | bytes 2097152 | tf_op jit(solution)/shard_map/reshape | solution.py:357
  136.8 0.7 bitcast_reduce_fusion
  (7 shorter events, 0.1 us)
Async XLA Ops:
  0.6 12.1 %copy-start = (bf16[128,4096]{1,0:T(8,128)(2,1)S(1)}, bf16[128,4096]{1,0:T(8,128)(2,1)}, u32[]{:S(2)}) copy-start(bf16[128,4096]{1,0:T(8,128)(2,1)} %param.13) | copy-start | bytes 3145732
  5.5 30.7 %all-to-all-start = ((bf16[32,112,128]{2,1,0:T(8,128)(2,1)}), bf16[32,112,128]{2,1,0:T(8,128)(2,1)S(1)}, u32[]{:S(2)}, u32[]{:S(2)}) async-start(bf16[32,112,128]{2,1,0:T(8,128)(2,1)} %pad_maximum_fusion), calls=%async_computation | async-start | bytes 1835008 | tf_op jit(solution)/shard_map/all_to_all | solution.py:347
  21.9 18.0 %copy-start.1 = (bf16[3,256]{1,0:T(4,128)(2,1)S(1)}, bf16[3,256]{1,0:T(4,128)(2,1)}, u32[]{:S(2)}) copy-start(bf16[3,256]{1,0:T(4,128)(2,1)} %param.11) | copy-start | bytes 4612
  36.2 29.9 %all-to-all-start.1 = ((f32[32,64,128]{2,1,0:T(8,128)}), f32[32,64,128]{2,1,0:T(8,128)S(1)}, u32[]{:S(2)}, u32[]{:S(2)}) async-start(f32[32,64,128]{2,1,0:T(8,128)} %bitcast.38), calls=%async_computation.1 | async-start | bytes 2097152 | tf_op jit(solution)/shard_map/all_to_all | solution.py:347

commit v2 on v1

--- a/solution.py
+++ b/solution.py
@@ -201,52 +201,76 @@
     return total + jnp.concatenate([last * u[half:], last * u[:half]], axis=0)
 
 
-def head_kernel(pk_ref, g_ref, meta_ref, taps_ref, out_ref, u_ref, du_ref, gext_ref):
+def load(ref, i, start, rows):
+    parts = [ref[i * BLOCKS + j, start : start + rows, :] for j in range(BLOCKS)]
+    return jnp.concatenate(parts, axis=1)
+
+
+def store(ref, i, start, x):
+    width = ref.shape[2]
+    for j in range(BLOCKS):
+        ref[i * BLOCKS + j, start : start + x.shape[0], :] = x[:, j * width : (j + 1) * width]
+
+
+def key_rows(pk_ref, i):
+    return load(pk_ref, i, FD, FD) * jnp.asarray(0.5, bf16)
+
+
+def value_rows(pk_ref, i):
+    channels = pk_ref.shape[1] - V_ROW
+    values = load(pk_ref, i, V_ROW, channels)
+    ones = lax.broadcasted_iota(jnp.int32, (FD, values.shape[1]), 0) == 0
+    return jnp.concatenate([values, ones.astype(bf16)], axis=0)
+
+
+def lanes(i, size):
+    return pl.ds(pl.multiple_of(i * size, size), size)
+
+
+def ending_kernel(pk_ref, meta_ref, state_ref):
+    size = BLOCKS * pk_ref.shape[2]
+
+    def step(i, state):
+        tail = meta_ref[8:9, lanes(i, size)]
+        feat_k = split(phi(key_rows(pk_ref, i).astype(f32)) * tail)
+        vext = value_rows(pk_ref, i)
+        return state + dot(vext, feat_k[0], NT) + dot(vext, feat_k[1], NT)
+
+    start = jnp.zeros(state_ref.shape, f32)
+    state_ref[...] = lax.fori_loop(0, pk_ref.shape[0] // BLOCKS, step, start)
+
+
+def forward_kernel(
+    pk_ref, g_ref, meta_ref, taps_ref, edge_ref, state_ref, part_ref, du_ref, inc_ref, pay_ref, u_ref
+):
     blocks, width = pk_ref.shape[0], pk_ref.shape[2]
     channels = g_ref.shape[1]
-    ext = channels + FD
-    seq = blocks * width
+    ext, nf = state_ref.shape
     size = BLOCKS * width
-    chunks = blocks // BLOCKS
-    nf = (FD // 2 + 2) * FD
-
-    def load(ref, i, start, rows):
-        parts = [ref[i * BLOCKS + j, start : start + rows, :] for j in range(BLOCKS)]
-        return jnp.concatenate(parts, axis=1)
-
-    def store(i, start, x, add):
-        for j in range(BLOCKS):
-            part = x[:, j * width : (j + 1) * width]
-            rows = pl.ds(start, x.shape[0])
-            if add:
-                part = part + out_ref[i * BLOCKS + j, rows, :]
-            out_ref[i * BLOCKS + j, rows, :] = part
-
-    raw = jnp.concatenate([pk_ref[j, 0:FD, :].astype(f32) for j in range(blocks)], axis=1) * 0.5
+
+    raw = [pk_ref[j, 0:FD, :].astype(f32) for j in range(blocks)]
+    raw = jnp.concatenate([edge_ref[...].astype(f32)] + raw, axis=1) * 0.5
     u_ref[...] = (
-        taps_ref[:, 0:1] * raw
-        + taps_ref[:, 1:2] * pltpu.roll(raw, 1, 1) * meta_ref[4:5, :]
-        + taps_ref[:, 2:3] * pltpu.roll(raw, 2, 1) * meta_ref[5:6, :]
+        taps_ref[:, 0:1] * raw[:, width:]
+        + taps_ref[:, 1:2] * pltpu.roll(raw, 1, 1)[:, width:] * meta_ref[4:5, :]
+        + taps_ref[:, 2:3] * pltpu.roll(raw, 2, 1)[:, width:] * meta_ref[5:6, :]
     )
     causal = lax.broadcasted_iota(jnp.int32, (size, size), 0) <= lax.broadcasted_iota(
         jnp.int32, (size, size), 1
     )
-    ones_rows = (lax.broadcasted_iota(jnp.int32, (FD, size), 0) == 0).astype(bf16)
-
-    def value_rows(i):
-        return jnp.concatenate([load(pk_ref, i, V_ROW, channels), ones_rows], axis=0)
-
-    def forward(i, state):
-        span = pl.ds(pl.multiple_of(i * size, size), size)
+
+    def step(i, carried):
+        state, leading = carried
+        span = lanes(i, size)
         u = u_ref[:, span]
-        w16 = load(pk_ref, i, FD, FD) * jnp.asarray(0.5, bf16)
-        w = w16.astype(f32)
-        vext = value_rows(i)
+        w16 = key_rows(pk_ref, i)
+        vext = value_rows(pk_ref, i)
         g = load(g_ref, i, 0, channels)
         seg = meta_ref[0:1, span]
         carry = meta_ref[1:2, span]
         tail = meta_ref[2:3, span]
         keep = meta_ref[3:4, span][:, 0:1]
+        first = meta_ref[9:10, span][:, 0:1]
         seg_t = jnp.broadcast_to(seg, (size, size))
         allowed = jnp.where(causal & (seg_t == seg_t.T), 1.0, 0.0)
         us = split(u)
@@ -260,105 +284,137 @@
         gp = g * inverse
         dden = -jnp.sum(gp * numer[:channels], axis=0, keepdims=True) * inverse
         gext = jnp.concatenate([gp, dden, jnp.zeros((FD - 1, size), f32)], axis=0)
-        gext_ref[:, span] = gext
         gs = split(gext)
         dx = split(slope * (dot(vext, gs[0], TN) + dot(vext, gs[1], TN)))
         du = dot(w16, dx[0], NN) + dot(w16, dx[1], NN)
         dw = dot3(us, dx, NT)
         dv = dot3((gs[0][:channels], gs[1][:channels]), p, NT)
         du_ref[:, span] = du + phi_pullback(u, dot3(states, gs, TN) * carry)
-        store(i, channels + FD, dw, False)
-        store(i, 0, dv, False)
-        feat_k = split(phi(w) * tail)
-        return keep * state + dot(vext, feat_k[0], NT) + dot(vext, feat_k[1], NT)
-
-    lax.fori_loop(0, chunks, forward, jnp.zeros((ext, nf), f32))
-
-    def backward(step, adjoint):
-        i = chunks - 1 - step
-        span = pl.ds(pl.multiple_of(i * size, size), size)
-        w = (load(pk_ref, i, FD, FD) * jnp.asarray(0.5, bf16)).astype(f32)
-        vext = value_rows(i)
+        store(part_ref, i, 0, dv)
+        store(part_ref, i, channels, dw)
+        inc = dot3(gs, feat_q, NT)
+        inc_ref[i] = inc
+        feat_k = split(phi(key_rows(pk_ref, i).astype(f32)) * tail)
+        state = keep * state + dot(vext, feat_k[0], NT) + dot(vext, feat_k[1], NT)
+        return state, leading + first * inc
+
+    start = (state_ref[...], jnp.zeros((ext, nf), f32))
+    _, leading = lax.fori_loop(0, blocks // BLOCKS, step, start)
+    pay_ref[0:ext, :] = leading
+    pay_ref[ext : ext + FD, :] = jnp.zeros((FD, nf), f32)
+    pay_ref[ext : ext + FD, 0:width] = du_ref[:, 0:width]
+
+
+def backward_kernel(pk_ref, meta_ref, taps_ref, part_ref, du_ref, inc_ref, pay_ref, out_ref):
+    blocks, width = pk_ref.shape[0], pk_ref.shape[2]
+    ext, nf = inc_ref.shape[1:]
+    channels = ext - FD
+    size = BLOCKS * width
+    chunks = blocks // BLOCKS
+
+    def step(count, adjoint):
+        i = chunks - 1 - count
+        span = lanes(i, size)
+        w = key_rows(pk_ref, i).astype(f32)
+        vext = value_rows(pk_ref, i)
         tail = meta_ref[2:3, span]
         keep = meta_ref[3:4, span][:, 0:1]
         adj = split(adjoint)
         feat_k = split(phi(w) * tail)
         dfeat = (dot(adj[0], vext, TN) + dot(adj[1], vext, TN)) * tail
-        old = load(out_ref, i, channels + FD, FD)
-        store(i, channels + FD, 0.5 * (old + phi_pullback(w, dfeat)), False)
-        store(i, 0, dot3((adj[0][:channels], adj[1][:channels]), feat_k, NN), True)
-        feat_q = split(phi(u_ref[:, span]) * meta_ref[1:2, span])
-        return keep * adjoint + dot3(split(gext_ref[:, span]), feat_q, NT)
-
-    lax.fori_loop(0, chunks, backward, jnp.zeros((ext, nf), f32))
-    du = du_ref[...] * 0.5
+        dw = load(part_ref, i, channels, FD) + phi_pullback(w, dfeat)
+        store(out_ref, i, channels + FD, 0.5 * dw)
+        dv = dot3((adj[0][:channels], adj[1][:channels]), feat_k, NN)
+        store(out_ref, i, 0, load(part_ref, i, 0, channels) + dv)
+        return keep * adjoint + inc_ref[i]
+
+    lax.fori_loop(0, chunks, step, pay_ref[0:ext, :])
+    du = jnp.concatenate([du_ref[...], pay_ref[ext : ext + FD, 0:width]], axis=1) * 0.5
+    seq, total = blocks * width, (blocks + 1) * width
     dq = (
-        taps_ref[:, 0:1] * du
-        + taps_ref[:, 1:2] * pltpu.roll(du, seq - 1, 1) * meta_ref[6:7, :]
-        + taps_ref[:, 2:3] * pltpu.roll(du, seq - 2, 1) * meta_ref[7:8, :]
+        taps_ref[:, 0:1] * du[:, :seq]
+        + taps_ref[:, 1:2] * pltpu.roll(du, total - 1, 1)[:, :seq] * meta_ref[6:7, :]
+        + taps_ref[:, 2:3] * pltpu.roll(du, total - 2, 1)[:, :seq] * meta_ref[7:8, :]
     )
     for j in range(blocks):
         out_ref[j, channels : channels + FD, :] = dq[:, j * width : (j + 1) * width]
 
 
-def head_call(pk, g, meta, taps):
-    blocks, _, width = pk.shape
-    channels = g.shape[1]
+def call(kernel, args, outs, scratch=(), flops=0):
+    shapes = [jax.ShapeDtypeStruct(shape, f32) for shape in outs]
     return pl.pallas_call(
-        head_kernel,
-        out_shape=jax.ShapeDtypeStruct((blocks, channels + 2 * FD, width), f32),
-        in_specs=[pl.BlockSpec(memory_space=pltpu.VMEM)] * 4,
-        out_specs=pl.BlockSpec(memory_space=pltpu.VMEM),
-        scratch_shapes=[
-            pltpu.VMEM((FD, blocks * width), f32),
-            pltpu.VMEM((FD, blocks * width), f32),
-            pltpu.VMEM((channels + FD, blocks * width), f32),
-        ],
+        kernel,
+        out_shape=shapes,
+        in_specs=[pl.BlockSpec(memory_space=pltpu.VMEM)] * len(args),
+        out_specs=[pl.BlockSpec(memory_space=pltpu.VMEM)] * len(outs),
+        scratch_shapes=[pltpu.VMEM(shape, f32) for shape in scratch],
         compiler_params=pltpu.CompilerParams(vmem_limit_bytes=40 * 2**20),
-    )(pk, g, meta, taps)
-
-
-def meta_rows(pk):
-    blocks, _, width = pk.shape
+        cost_estimate=pl.CostEstimate(flops=flops, bytes_accessed=2**21, transcendentals=0),
+    )(*args)
+
+
+def meta_rows(pk, edge_before, edge_after):
+    width = pk.shape[2]
     size = BLOCKS * width
     seg = pk[:, SEG_ROW, :].astype(f32).reshape(-1)
+    earlier = edge_before[SEG_ROW].astype(f32)
+    later = edge_after[SEG_ROW].astype(f32)
     last = jnp.repeat(seg[size - 1 :: size], size)
-    before = jnp.concatenate([jnp.full((size,), -1.0, f32), last[:-size]])
+    open_here = earlier[width - 1]
+    before = jnp.concatenate([jnp.full((size,), open_here), last[:-size]])
     same = lambda a, b: (a == b).astype(f32)
-    late = lambda d: same(jnp.pad(seg, (d, 0), constant_values=-1.0)[:-d], seg)
-    soon = lambda d: same(jnp.pad(seg, (0, d), constant_values=-1.0)[d:], seg)
+    late = lambda d: same(jnp.concatenate([earlier[width - d :], seg[:-d]]), seg)
+    soon = lambda d: same(jnp.concatenate([seg[d:], later[:d]]), seg)
     rows = [seg, same(seg, before), same(seg, last), same(before, last)]
-    return jnp.stack(rows + [late(1), late(2), soon(1), soon(2)])
-
-
-def pack(queries, keys, values, seg_ids, size):
+    rows += [late(1), late(2), soon(1), soon(2)]
+    rows += [same(seg, seg[-1]), same(before, open_here)]
+    return jnp.pad(jnp.stack(rows), ((0, 6), (0, 0)))
+
+
+def pack(queries, keys, values, seg_ids):
     heads, length = queries.shape[0] // FD, queries.shape[1]
-    share = size // heads
-    twice = lambda x: jnp.repeat(x.reshape(heads, FD, length), share, axis=0)
-    seg = jnp.broadcast_to(seg_ids.astype(bf16), (size, FD, length))
-    rows = values.T.reshape(size, -1, length)
-    return jnp.concatenate([twice(queries), twice(keys), seg, rows], axis=1)
+    shaped = lambda x: x.reshape(heads, -1, length)
+    seg = jnp.broadcast_to((seg_ids + 1).astype(bf16), (heads, FD, length))
+    return jnp.concatenate([shaped(queries), shaped(keys), seg, shaped(values.T)], axis=1)
 
 
 def by_heads(queries, keys, values, seg_ids, conv_weight, out_weight, out_grad):
-    size = lax.axis_size("ctx")
     heads, length = queries.shape[0] // FD, queries.shape[1]
-    share = size // heads
-    swap = lambda x: lax.all_to_all(x, "ctx", 0, 0)
-    pk = swap(pack(queries, keys, values, seg_ids, size))
+    groups = [[half * heads + h for h in range(heads)] for half in (0, 1)]
+    swap = lambda x: lax.all_to_all(x, "ctx", 0, 0, axis_index_groups=groups)
+    onward = lambda x: lax.ppermute(x, "ctx", [(h, h + heads) for h in range(heads)])
+    back = lambda x: lax.ppermute(x, "ctx", [(h + heads, h) for h in range(heads)])
+    pk = swap(pack(queries, keys, values, seg_ids))
     grad_attn = lax.dot_general(out_weight, out_grad, NT, preferred_element_type=f32)
-    g = swap(grad_attn.reshape(size, -1, length))
-    head = lax.axis_index("ctx") // share
+    g = swap(grad_attn.reshape(heads, -1, length))
+    channels = g.shape[1]
+    head = lax.rem(lax.axis_index("ctx"), heads)
     taps = lax.dynamic_slice_in_dim(conv_weight.astype(f32).T, head * FD, FD, 0)
     taps = jnp.pad(taps, ((0, 0), (0, 128 - taps.shape[1])))
-    out = swap(head_call(pk, g, meta_rows(pk), taps))
-    channels = g.shape[1]
-    joined = lambda x: x.reshape(heads, share, FD, length).sum(1).reshape(heads * FD, length)
-    grad_values = out[:, :channels].reshape(-1, length).T
+    edge_before = onward(pk[-1, :V_ROW])
+    edge_after = back(pk[0, :V_ROW])
+    meta = meta_rows(pk, edge_before, edge_after)
+    ext, nf = channels + FD, (FD // 2 + 2) * FD
+    seq = heads * length
+    (ending,) = call(ending_kernel, (pk, meta), [(ext, nf)], flops=4 * ext * nf * seq)
+    part, du, inc, pay = call(
+        forward_kernel,
+        (pk, g, meta, taps, edge_before[:FD], onward(ending)),
+        [(heads, ext, length), (FD, seq), (heads // BLOCKS, ext, nf), (ext + FD, nf)],
+        [(FD, seq)],
+        flops=40 * ext * nf * seq,
+    )
+    (out,) = call(
+        backward_kernel,
+        (pk, meta, taps, part, du, inc, back(pay)),
+        [(heads, ext + FD, length)],
+        flops=10 * ext * nf * seq,
+    )
+    out = swap(out)
     return (
-        joined(out[:, channels : channels + FD]),
-        joined(out[:, channels + FD :]),
-        grad_values,
+        out[:, channels : channels + FD].reshape(heads * FD, length),
+        out[:, channels + FD :].reshape(heads * FD, length),
+        out[:, :channels].reshape(-1, length).T,
     )
 
 

time: 138 us -> 103 us (0.75)
  blocking collectives: 41.4 us -> 22.9 us
  waiting for transfers between devices: 39.7 us -> 22 us
  starting transfers between devices: 10.9 us -> 22.3 us
  Pallas kernels: 25.7 us -> 15.8 us
  other arithmetic: 2.67 us -> 4.72 us
  local copies, waits for them, and re-layouts: 7.22 us -> 5.32 us
    all_to_all x2, waiting for transfers between devices: 39.7 us -> 3.53 us  [by_heads(): swap = lambda x: lax.all_to_all(x, 'ctx', 0, 0, axis_index_groups=groups)]
    all_to_all x1, blocking collectives: 41.4 us -> 22.9 us  [by_heads(): swap = lambda x: lax.all_to_all(x, 'ctx', 0, 0, axis_index_groups=groups)]
    ppermute x0 -> x4, waiting for transfers between devices: none -> 18.5 us  [the longest x2 10.3 us: by_heads(): lax.ppermute(x, 'ctx', [(h + heads, h) for h in range(heads)])]
    ppermute x0 -> x4, starting transfers between devices: none -> 12.4 us  [the longest x2 9.78 us: by_heads(): lax.ppermute(x, 'ctx', [(h, h + heads) for h in range(heads)])]
    pallas_call x1 -> x3, Pallas kernels: 25.7 us -> 15.8 us  [call(): pl.pallas_call(kernel, out_shape=shapes, in_specs=[pl.BlockSpec(memory_sp...]
    broadcast_in_dim x3 -> x1, local copies, waits for them, and re-layouts: 1.74 us -> 0.01 us  [pack(): seg = jnp.broadcast_to((seg_ids + 1).astype(bf16), (heads, FD, length))]
    convert_element_type x1, other arithmetic: 0.02 us -> 1.4 us  [meta_rows(): same = lambda a, b: (a == b).astype(f32)]
  transfers between devices with their start and end apart: 2 -> 6, of which waited for: 2 -> 4; matrix products, arithmetic and copies ran while one was open for 7% -> 13% of each run, Pallas kernels for 0% -> 2%
where the time goes in v2:
time: 103 us
  blocking collectives  22.9 us (22%)
  starting transfers between devices  22.3 us (22%)
  waiting for transfers between devices  22 us (21%)
  Pallas kernels  15.8 us (15%)
  matrix products  9.11 us (9%)
  local copies, waits for them, and re-layouts  5.32 us (5%)
  other arithmetic  4.72 us (5%)
    all_to_all x1, blocking collectives, by_heads(): swap = lambda x: lax.all_to_all(x, 'ctx', 0, 0, axis_index_groups=groups)  22.9 us
    pallas_call x3, Pallas kernels, call(): pl.pallas_call(kernel, out_shape=shapes, in_specs=[pl.BlockSpec(memory_sp...  15.8 us
    ppermute x2, waiting for transfers between devices, by_heads(): lax.ppermute(x, 'ctx', [(h + heads, h) for h in range(heads)])  10.3 us
    all_to_all x2, starting transfers between devices, by_heads(): swap = lambda x: lax.all_to_all(x, 'ctx', 0, 0, axis_index_groups=groups)  9.94 us
    ppermute x2, starting transfers between devices, by_heads(): lax.ppermute(x, 'ctx', [(h, h + heads) for h in range(heads)])  9.78 us
    dot_general x1, matrix products, by_heads(): lax.dot_general(out_weight, out_grad, NT, preferred_element_type=f32)  9.11 us
    ppermute x2, waiting for transfers between devices, by_heads(): lax.ppermute(x, 'ctx', [(h, h + heads) for h in range(heads)])  8.18 us
    all_to_all x2, waiting for transfers between devices, by_heads(): swap = lambda x: lax.all_to_all(x, 'ctx', 0, 0, axis_index_groups=groups)  3.53 us
  transfers between devices with their start and end apart: 6, of which 4 were waited for; matrix products, arithmetic and copies ran while one was open for 13% of the time, Pallas kernels for 2%

profile of v2, /device:TPU:0, one launch (start us, length us, event | category | flops | bytes accessed | tf_op | source)
XLA Modules:
  0.0 102.9 jit_solution(4906594466733811065)
XLA Ops:
  0.6 0.0 copy-start
  0.6 0.7 add_convert_fusion
  1.4 1.3 %copy.10 = bf16[2048,128]{1,0:T(8,128)(2,1)S(1)} copy(bf16[2048,128]{0,1:T(8,128)(2,1)} %bitcast.48) | data formatting | bytes 1048576 | tf_op jit(solution)/shard_map/transpose | solution.py:378
  2.7 1.8 %pad_maximum_fusion = bf16[16,176,128]{2,1,0:T(8,128)(2,1)} fusion(bf16[16,128,128]{2,1,0:T(8,128)(2,1)S(1)} %bitcast.45, bf16[16,16,128]{2,1,0:T(8,128)(2,1)S(1)} %broadcast_in_dim.9, bf16[16,16,128]{2,1,0:T(8,128)(2,1)} %bitcast.56, bf16[16,16,128]{2,1,0:T(8,128)(2,1)} %bitcast.57), kind=kLoop, calls=%fused_computation | loop fusion | flops 2883584 | bytes 1441792 | tf_op jit(solution)/shard_map/concatenate | solution.py:378
  4.5 6.3 %all-to-all-start = ((bf16[16,176,128]{2,1,0:T(8,128)(2,1)}), bf16[16,176,128]{2,1,0:T(8,128)(2,1)S(1)}, u32[]{:S(2)}, u32[]{:S(2)}) async-start(bf16[16,176,128]{2,1,0:T(8,128)(2,1)} %pad_maximum_fusion), calls=%async_computation | async-start | bytes 1441792 | tf_op jit(solution)/shard_map/all_to_all | solution.py:384
  10.9 0.0 copy-done
  10.9 9.1 %fusion.4 = f32[2048,128]{1,0:T(8,128)} fusion(bf16[2048,4096]{1,0:T(8,128)(2,1)} %param.12, bf16[128,4096]{1,0:T(8,128)(2,1)S(1)} %copy-done), kind=kOutput, calls=%fused_computation.23 | convolution fusion | flops 2147483648 | bytes 18874368 | tf_op jit(solution)/shard_map/dot_general | solution.py:388
  20.0 3.5 %all-to-all-done.pk_ref = bf16[16,176,128]{2,1,0:T(8,128)(2,1)S(1)} async-done(((bf16[16,176,128]{2,1,0:T(8,128)(2,1)}), bf16[16,176,128]{2,1,0:T(8,128)(2,1)S(1)}, u32[]{:S(2)}, u32[]{:S(2)}) %all-to-all-start) | async-done | bytes 720928 | tf_op jit(solution)/shard_map/all_to_all | solution.py:384
  23.5 3.7 %all-to-all-start.1 = ((f32[16,128,128]{2,1,0:T(8,128)}), f32[16,128,128]{2,1,0:T(8,128)S(1)}, u32[]{:S(2)}, u32[]{:S(2)}) async-start(f32[16,128,128]{2,1,0:T(8,128)} %bitcast.46), calls=%async_computation.1 | async-start | bytes 2097152 | tf_op jit(solution)/shard_map/all_to_all | solution.py:384
  27.2 0.0 copy-start.1
  27.2 0.1 slice.70
  27.3 4.5 %collective-permute-start = (bf16[48,128]{1,0:T(8,128)(2,1)S(1)}, bf16[48,128]{1,0:T(8,128)(2,1)S(1)}, u32[]{:S(2)}, u32[]{:S(2)}) collective-permute-start(bf16[48,128]{1,0:T(8,128)(2,1)S(1)} %get-tuple-element.20), channel_id=1, source_target_pairs={{0,16},{1,17},{2,18},{3,19},{4,20},{5,21},{6,22},{7,23},{8,24},{9,... | collective-permute-start | bytes 36872 | tf_op jit(solution)/shard_map/ppermute | solution.py:385
  31.8 0.1 fusion.3
  31.9 0.1 fusion.2
  31.9 0.1 broadcast_bitcast_fusion
  32.0 0.6 slice.99
  32.6 0.1 broadcast_in_dim.10
  32.7 1.3 %collective-permute-start.1 = (bf16[48,128]{1,0:T(8,128)(2,1)S(1)}, bf16[48,128]{1,0:T(8,128)(2,1)S(1)}, u32[]{:S(2)}, u32[]{:S(2)}) collective-permute-start(bf16[48,128]{1,0:T(8,128)(2,1)S(1)} %get-tuple-element.19), channel_id=1, source_target_pairs={{16,0},{17,1},{18,2},{19,3},{20,4},{21,5},{22,6},{23,7},{24,8},{25... | collective-permute-start | bytes 36872 | tf_op jit(solution)/shard_map/ppermute | solution.py:386
  34.0 5.6 %collective-permute-done = bf16[48,128]{1,0:T(8,128)(2,1)S(1)} collective-permute-done((bf16[48,128]{1,0:T(8,128)(2,1)S(1)}, bf16[48,128]{1,0:T(8,128)(2,1)S(1)}, u32[]{:S(2)}, u32[]{:S(2)}) %collective-permute-start) | collective-permute-done | bytes 12320 | tf_op jit(solution)/shard_map/ppermute | solution.py:385
  39.6 0.6 slice.75
  40.1 0.1 slice.77
  40.2 0.0 collective-permute-done.1
  40.2 0.7 compare_convert_fusion.6
  40.9 1.4 %compare_convert_fusion = (f32[1,2048]{1,0:T(1,128)S(1)}, f32[1,2048]{1,0:T(1,128)S(1)}, f32[1,2048]{1,0:T(1,128)S(1)}, f32[1,2048]{1,0:T(1,128)S(1)}, f32[1,2048]{1,0:T(1,128)S(1)}, /*index=5*/f32[1,2048]{1,0:T(1,128)S(1)}) fusion(f32[]{:T(128)} %bitcast.15, bf16[16,176,128]{2,1,0:T(8,128)(2,1)S(1)} %all-to-all-done.pk_ref, f32[1,2]{1,0:T(1,128)S(1)} %bitcast.68, ...), kind=kLoop, calls=%fused_computation.1 | loop fusion | flops 34816 | bytes 94212 | tf_op jit(solution)/shard_map/convert_element_type | solution.py:365
  42.3 0.1 stack.33
  42.4 1.7 %shard_map.94 = f32[144,160]{1,0:T(8,128)S(1)} custom-call(bf16[16,176,128]{2,1,0:T(8,128)(2,1)S(1)} %all-to-all-done.pk_ref, f32[16,2048]{1,0:T(8,128)S(1)} %pad.9.meta_ref), custom_call_target="tpu_custom_call" | custom-call | flops 188743680 | bytes 2097152 | tf_op jit(solution)/shard_map/pallas_call | solution.py:345
  44.2 5.3 %collective-permute-start.2 = (f32[144,160]{1,0:T(8,128)S(1)}, f32[144,160]{1,0:T(8,128)S(1)}, u32[]{:S(2)}, u32[]{:S(2)}) collective-permute-start(f32[144,160]{1,0:T(8,128)S(1)} %shard_map.94), channel_id=1, source_target_pairs={{0,16},{1,17},{2,18},{3,19},{4,20},{5,21},{6,22},{7,23},{8,24},{9,... | collective-permute-start | bytes 276488 | tf_op jit(solution)/shard_map/ppermute | solution.py:385
  49.5 0.0 copy-done.1
  49.5 0.1 dynamic-slice_convert_fusion
  49.6 0.1 copy.13
  49.7 2.6 %collective-permute-done.2.state_ref = f32[144,160]{1,0:T(8,128)S(1)} collective-permute-done((f32[144,160]{1,0:T(8,128)S(1)}, f32[144,160]{1,0:T(8,128)S(1)}, u32[]{:S(2)}, u32[]{:S(2)}) %collective-permute-start.2) | collective-permute-done | bytes 92192 | tf_op jit(solution)/shard_map/ppermute | solution.py:385
  52.3 0.0 all-to-all-done.1.g_ref
  52.3 11.4 %shard_map.95 = (f32[16,144,128]{2,1,0:T(8,128)S(1)}, f32[16,2048]{1,0:T(8,128)S(1)}, f32[8,144,160]{2,1,0:T(8,128)S(1)}, f32[160,160]{1,0:T(8,128)S(1)}) custom-call(bf16[16,176,128]{2,1,0:T(8,128)(2,1)S(1)} %all-to-all-done.pk_ref, f32[16,128,128]{2,1,0:T(8,128)S(1)} %all-to-all-done.1.g_ref, f32[16,2048]{1,0:T(8,128)S(1)} %pad.9.meta_ref, ...), custom_call_target="tpu_custom_call" | custom-call | flops 1887436800 | bytes 2097152 | tf_op jit(solution)/shard_map/pallas_call | solution.py:345
  63.7 1.3 %collective-permute-start.3 = (f32[160,160]{1,0:T(8,128)S(1)}, f32[160,160]{1,0:T(8,128)S(1)}, u32[]{:S(2)}, u32[]{:S(2)}) collective-permute-start(f32[160,160]{1,0:T(8,128)S(1)} %get-tuple-element.10), channel_id=1, source_target_pairs={{16,0},{17,1},{18,2},{19,3},{20,4},{21,5},{22,6},{23,7},{24,8},{25... | collective-permute-start | bytes 307208 | tf_op jit(solution)/shard_map/ppermute | solution.py:386
  65.0 10.3 %collective-permute-done.3.pay_ref = f32[160,160]{1,0:T(8,128)S(1)} collective-permute-done((f32[160,160]{1,0:T(8,128)S(1)}, f32[160,160]{1,0:T(8,128)S(1)}, u32[]{:S(2)}, u32[]{:S(2)}) %collective-permute-start.3) | collective-permute-done | bytes 102432 | tf_op jit(solution)/shard_map/ppermute | solution.py:386
  75.3 2.6 %shard_map.96 = f32[16,160,128]{2,1,0:T(8,128)S(1)} custom-call(bf16[16,176,128]{2,1,0:T(8,128)(2,1)S(1)} %all-to-all-done.pk_ref, f32[16,2048]{1,0:T(8,128)S(1)} %pad.9.meta_ref, f32[16,128]{1,0:T(8,128)S(1)} %pad.10.taps_ref, f32[16,144,128]{2,1,0:T(8,128)S(1)} %get-tuple-element.7.part_ref, f32[16,2048]{1,0:T(8,128)S(1)} %get-tuple-element.8.du_ref, ...), custom_call_target="tpu_custom_call" | custom-call | flops 471859200 | bytes 2097152 | tf_op jit(solution)/shard_map/pallas_call | solution.py:345
  78.0 22.9 %all_to_all.15 = f32[16,160,128]{2,1,0:T(8,128)S(1)} all-to-all(f32[16,160,128]{2,1,0:T(8,128)S(1)} %shard_map.96), channel_id=1, replica_groups={{0,1,2,3,4,5,6,7,8,9,10,11,12,13,14,15},{16,17,18,19,20,21,22,23,24,25,..., dimensions={0} | all-to-all | bytes 2621440 | tf_op jit(solution)/shard_map/all_to_all | solution.py:384
  100.8 0.1 slice.103
  100.9 1.3 %copy.12 = f32[2048,128]{0,1:T(8,128)} copy(f32[2048,128]{1,0:T(8,128)S(1)} %bitcast.44) | data formatting | bytes 2097152 | tf_op jit(solution)/shard_map/reshape | solution.py:417
  102.2 0.7 fusion.1
  (11 shorter events, 0.1 us)
Async XLA Ops:
  0.6 10.2 %copy-start = (bf16[128,4096]{1,0:T(8,128)(2,1)S(1)}, bf16[128,4096]{1,0:T(8,128)(2,1)}, u32[]{:S(2)}) copy-start(bf16[128,4096]{1,0:T(8,128)(2,1)} %param.13) | copy-start | bytes 3145732
  4.5 18.9 %all-to-all-start = ((bf16[16,176,128]{2,1,0:T(8,128)(2,1)}), bf16[16,176,128]{2,1,0:T(8,128)(2,1)S(1)}, u32[]{:S(2)}, u32[]{:S(2)}) async-start(bf16[16,176,128]{2,1,0:T(8,128)(2,1)} %pad_maximum_fusion), calls=%async_computation | async-start | bytes 1441792 | tf_op jit(solution)/shard_map/all_to_all | solution.py:384
  23.5 28.8 %all-to-all-start.1 = ((f32[16,128,128]{2,1,0:T(8,128)}), f32[16,128,128]{2,1,0:T(8,128)S(1)}, u32[]{:S(2)}, u32[]{:S(2)}) async-start(f32[16,128,128]{2,1,0:T(8,128)} %bitcast.46), calls=%async_computation.1 | async-start | bytes 2097152 | tf_op jit(solution)/shard_map/all_to_all | solution.py:384
  27.2 22.3 %copy-start.1 = (bf16[3,256]{1,0:T(4,128)(2,1)S(1)}, bf16[3,256]{1,0:T(4,128)(2,1)}, u32[]{:S(2)}) copy-start(bf16[3,256]{1,0:T(4,128)(2,1)} %param.11) | copy-start | bytes 4612
  27.3 12.3 %collective-permute-start = (bf16[48,128]{1,0:T(8,128)(2,1)S(1)}, bf16[48,128]{1,0:T(8,128)(2,1)S(1)}, u32[]{:S(2)}, u32[]{:S(2)}) collective-permute-start(bf16[48,128]{1,0:T(8,128)(2,1)S(1)} %get-tuple-element.20), channel_id=1, source_target_pairs={{0,16},{1,17},{2,18},{3,19},{4,20},{5,21},{6,22},{7,23},{8,24},{9,... | collective-permute-start | bytes 36872 | tf_op jit(solution)/shard_map/ppermute | solution.py:385
  32.7 7.5 %collective-permute-start.1 = (bf16[48,128]{1,0:T(8,128)(2,1)S(1)}, bf16[48,128]{1,0:T(8,128)(2,1)S(1)}, u32[]{:S(2)}, u32[]{:S(2)}) collective-permute-start(bf16[48,128]{1,0:T(8,128)(2,1)S(1)} %get-tuple-element.19), channel_id=1, source_target_pairs={{16,0},{17,1},{18,2},{19,3},{20,4},{21,5},{22,6},{23,7},{24,8},{25... | collective-permute-start | bytes 36872 | tf_op jit(solution)/shard_map/ppermute | solution.py:386
  44.2 8.1 %collective-permute-start.2 = (f32[144,160]{1,0:T(8,128)S(1)}, f32[144,160]{1,0:T(8,128)S(1)}, u32[]{:S(2)}, u32[]{:S(2)}) collective-permute-start(f32[144,160]{1,0:T(8,128)S(1)} %shard_map.94), channel_id=1, source_target_pairs={{0,16},{1,17},{2,18},{3,19},{4,20},{5,21},{6,22},{7,23},{8,24},{9,... | collective-permute-start | bytes 276488 | tf_op jit(solution)/shard_map/ppermute | solution.py:385
  63.7 11.6 %collective-permute-start.3 = (f32[160,160]{1,0:T(8,128)S(1)}, f32[160,160]{1,0:T(8,128)S(1)}, u32[]{:S(2)}, u32[]{:S(2)}) collective-permute-start(f32[160,160]{1,0:T(8,128)S(1)} %get-tuple-element.10), channel_id=1, source_target_pairs={{16,0},{17,1},{18,2},{19,3},{20,4},{21,5},{22,6},{23,7},{24,8},{25... | collective-permute-start | bytes 307208 | tf_op jit(solution)/shard_map/ppermute | solution.py:386

commit v3 on v2

--- a/solution.py
+++ b/solution.py
@@ -160,8 +160,7 @@
 NT = (((1,), (1,)), ((), ()))
 TN = (((0,), (0,)), ((), ()))
 BLOCKS = 2
-SEG_ROW = 2 * FD
-V_ROW = 3 * FD
+V_ROW = 2 * FD
 
 
 def split(x):
@@ -236,73 +235,98 @@
         vext = value_rows(pk_ref, i)
         return state + dot(vext, feat_k[0], NT) + dot(vext, feat_k[1], NT)
 
-    start = jnp.zeros(state_ref.shape, f32)
-    state_ref[...] = lax.fori_loop(0, pk_ref.shape[0] // BLOCKS, step, start)
+    blocks, width = pk_ref.shape[0], pk_ref.shape[2]
+    ext, nf = state_ref.shape[0] - FD, state_ref.shape[1]
+    state_ref[0:ext, :] = lax.fori_loop(0, blocks // BLOCKS, step, jnp.zeros((ext, nf), f32))
+    state_ref[ext : ext + FD, :] = jnp.zeros((FD, nf), f32)
+    state_ref[ext : ext + FD, 0:width] = pk_ref[blocks - 1, 0:FD, :].astype(f32)
+
+
+def attend(pk_ref, meta_ref, u_ref, i):
+    size = BLOCKS * pk_ref.shape[2]
+    span = lanes(i, size)
+    seg_t = jnp.broadcast_to(meta_ref[0:1, span], (size, size))
+    causal = lax.broadcasted_iota(jnp.int32, (size, size), 0) <= lax.broadcasted_iota(
+        jnp.int32, (size, size), 1
+    )
+    allowed = jnp.where(causal & (seg_t == seg_t.T), 1.0, 0.0)
+    us = split(u_ref[:, span])
+    w16 = key_rows(pk_ref, i)
+    x = dot(jnp.concatenate([w16, w16], axis=0), jnp.concatenate(us, axis=0), TN)
+    return allowed * (1.0 + x), split(allowed * (1.0 + x + 0.5 * x * x))
+
+
+def query_grad(pk_ref, meta_ref, u_ref, slope, gs, states, i):
+    span = lanes(i, BLOCKS * pk_ref.shape[2])
+    vext = value_rows(pk_ref, i)
+    w16 = key_rows(pk_ref, i)
+    dx = split(slope * (dot(vext, gs[0], TN) + dot(vext, gs[1], TN)))
+    dfeat = dot3(states, gs, TN) * meta_ref[1:2, span]
+    return dx, dot(w16, dx[0], NN) + dot(w16, dx[1], NN) + phi_pullback(u_ref[:, span], dfeat)
 
 
 def forward_kernel(
-    pk_ref, g_ref, meta_ref, taps_ref, edge_ref, state_ref, part_ref, du_ref, inc_ref, pay_ref, u_ref
+    pk_ref, g_ref, meta_ref, taps_ref, state_ref, u_ref, gext_ref, states_ref, inc_ref, pay_ref
 ):
     blocks, width = pk_ref.shape[0], pk_ref.shape[2]
     channels = g_ref.shape[1]
-    ext, nf = state_ref.shape
+    ext, nf = channels + FD, state_ref.shape[1]
     size = BLOCKS * width
 
     raw = [pk_ref[j, 0:FD, :].astype(f32) for j in range(blocks)]
-    raw = jnp.concatenate([edge_ref[...].astype(f32)] + raw, axis=1) * 0.5
+    raw = jnp.concatenate([state_ref[ext : ext + FD, 0:width]] + raw, axis=1) * 0.5
     u_ref[...] = (
         taps_ref[:, 0:1] * raw[:, width:]
         + taps_ref[:, 1:2] * pltpu.roll(raw, 1, 1)[:, width:] * meta_ref[4:5, :]
         + taps_ref[:, 2:3] * pltpu.roll(raw, 2, 1)[:, width:] * meta_ref[5:6, :]
     )
-    causal = lax.broadcasted_iota(jnp.int32, (size, size), 0) <= lax.broadcasted_iota(
-        jnp.int32, (size, size), 1
-    )
 
     def step(i, carried):
         state, leading = carried
         span = lanes(i, size)
-        u = u_ref[:, span]
-        w16 = key_rows(pk_ref, i)
         vext = value_rows(pk_ref, i)
-        g = load(g_ref, i, 0, channels)
-        seg = meta_ref[0:1, span]
-        carry = meta_ref[1:2, span]
-        tail = meta_ref[2:3, span]
         keep = meta_ref[3:4, span][:, 0:1]
         first = meta_ref[9:10, span][:, 0:1]
-        seg_t = jnp.broadcast_to(seg, (size, size))
-        allowed = jnp.where(causal & (seg_t == seg_t.T), 1.0, 0.0)
-        us = split(u)
-        x = dot(jnp.concatenate([w16, w16], axis=0), jnp.concatenate(us, axis=0), TN)
-        slope = allowed * (1.0 + x)
-        p = split(allowed * (1.0 + x + 0.5 * x * x))
-        feat_q = split(phi(u) * carry)
-        states = split(state)
-        numer = dot(vext, p[0], NN) + dot(vext, p[1], NN) + dot3(states, feat_q, NN)
+        _, p = attend(pk_ref, meta_ref, u_ref, i)
+        feat_q = split(phi(u_ref[:, span]) * meta_ref[1:2, span])
+        states_ref[i] = state
+        numer = dot(vext, p[0], NN) + dot(vext, p[1], NN) + dot3(split(state), feat_q, NN)
         inverse = 1.0 / numer[channels : channels + 1]
-        gp = g * inverse
+        gp = load(g_ref, i, 0, channels) * inverse
         dden = -jnp.sum(gp * numer[:channels], axis=0, keepdims=True) * inverse
         gext = jnp.concatenate([gp, dden, jnp.zeros((FD - 1, size), f32)], axis=0)
-        gs = split(gext)
-        dx = split(slope * (dot(vext, gs[0], TN) + dot(vext, gs[1], TN)))
-        du = dot(w16, dx[0], NN) + dot(w16, dx[1], NN)
-        dw = dot3(us, dx, NT)
-        dv = dot3((gs[0][:channels], gs[1][:channels]), p, NT)
-        du_ref[:, span] = du + phi_pullback(u, dot3(states, gs, TN) * carry)
-        store(part_ref, i, 0, dv)
-        store(part_ref, i, channels, dw)
-        inc = dot3(gs, feat_q, NT)
+        gext_ref[:, span] = gext
+        inc = dot3(split(gext), feat_q, NT)
         inc_ref[i] = inc
-        feat_k = split(phi(key_rows(pk_ref, i).astype(f32)) * tail)
+        feat_k = split(phi(key_rows(pk_ref, i).astype(f32)) * meta_ref[2:3, span])
         state = keep * state + dot(vext, feat_k[0], NT) + dot(vext, feat_k[1], NT)
         return state, leading + first * inc
 
-    start = (state_ref[...], jnp.zeros((ext, nf), f32))
+    start = (state_ref[0:ext, :], jnp.zeros((ext, nf), f32))
     _, leading = lax.fori_loop(0, blocks // BLOCKS, step, start)
+    slope, _ = attend(pk_ref, meta_ref, u_ref, 0)
+    gs = split(gext_ref[:, 0:size])
+    _, du = query_grad(pk_ref, meta_ref, u_ref, slope, gs, split(states_ref[0]), 0)
     pay_ref[0:ext, :] = leading
     pay_ref[ext : ext + FD, :] = jnp.zeros((FD, nf), f32)
-    pay_ref[ext : ext + FD, 0:width] = du_ref[:, 0:width]
+    pay_ref[ext : ext + FD, 0:width] = du[:, 0:width]
+
+
+def inner_kernel(pk_ref, meta_ref, u_ref, gext_ref, states_ref, part_ref, du_ref):
+    channels = gext_ref.shape[0] - FD
+    size = BLOCKS * pk_ref.shape[2]
+
+    def step(i, nothing):
+        span = lanes(i, size)
+        slope, p = attend(pk_ref, meta_ref, u_ref, i)
+        gs = split(gext_ref[:, span])
+        dx, du = query_grad(pk_ref, meta_ref, u_ref, slope, gs, split(states_ref[i]), i)
+        du_ref[:, span] = du
+        store(part_ref, i, 0, dot3((gs[0][:channels], gs[1][:channels]), p, NT))
+        store(part_ref, i, channels, dot3(split(u_ref[:, span]), dx, NT))
+        return nothing
+
+    lax.fori_loop(0, pk_ref.shape[0] // BLOCKS, step, 0)
 
 
 def backward_kernel(pk_ref, meta_ref, taps_ref, part_ref, du_ref, inc_ref, pay_ref, out_ref):
@@ -340,25 +364,21 @@
         out_ref[j, channels : channels + FD, :] = dq[:, j * width : (j + 1) * width]
 
 
-def call(kernel, args, outs, scratch=(), flops=0):
+def call(kernel, args, outs, flops):
     shapes = [jax.ShapeDtypeStruct(shape, f32) for shape in outs]
     return pl.pallas_call(
         kernel,
         out_shape=shapes,
         in_specs=[pl.BlockSpec(memory_space=pltpu.VMEM)] * len(args),
         out_specs=[pl.BlockSpec(memory_space=pltpu.VMEM)] * len(outs),
-        scratch_shapes=[pltpu.VMEM(shape, f32) for shape in scratch],
         compiler_params=pltpu.CompilerParams(vmem_limit_bytes=40 * 2**20),
         cost_estimate=pl.CostEstimate(flops=flops, bytes_accessed=2**21, transcendentals=0),
     )(*args)
 
 
-def meta_rows(pk, edge_before, edge_after):
-    width = pk.shape[2]
+def meta_rows(seg_ext, width):
     size = BLOCKS * width
-    seg = pk[:, SEG_ROW, :].astype(f32).reshape(-1)
-    earlier = edge_before[SEG_ROW].astype(f32)
-    later = edge_after[SEG_ROW].astype(f32)
+    earlier, seg, later = seg_ext[:width], seg_ext[width:-width], seg_ext[-width:]
     last = jnp.repeat(seg[size - 1 :: size], size)
     open_here = earlier[width - 1]
     before = jnp.concatenate([jnp.full((size,), open_here), last[:-size]])
@@ -371,11 +391,10 @@
     return jnp.pad(jnp.stack(rows), ((0, 6), (0, 0)))
 
 
-def pack(queries, keys, values, seg_ids):
+def pack(queries, keys, values):
     heads, length = queries.shape[0] // FD, queries.shape[1]
     shaped = lambda x: x.reshape(heads, -1, length)
-    seg = jnp.broadcast_to((seg_ids + 1).astype(bf16), (heads, FD, length))
-    return jnp.concatenate([shaped(queries), shaped(keys), seg, shaped(values.T)], axis=1)
+    return jnp.concatenate([shaped(queries), shaped(keys), shaped(values.T)], axis=1)
 
 
 def by_heads(queries, keys, values, seg_ids, conv_weight, out_weight, out_grad):
@@ -384,31 +403,35 @@
     swap = lambda x: lax.all_to_all(x, "ctx", 0, 0, axis_index_groups=groups)
     onward = lambda x: lax.ppermute(x, "ctx", [(h, h + heads) for h in range(heads)])
     back = lambda x: lax.ppermute(x, "ctx", [(h + heads, h) for h in range(heads)])
-    pk = swap(pack(queries, keys, values, seg_ids))
+    here = lax.axis_index("ctx")
+    seq = heads * length
+    pk = swap(pack(queries, keys, values))
+    everyone = jnp.pad(lax.all_gather(seg_ids, "ctx", tiled=True) + 1, (length, length))
+    seg_ext = lax.dynamic_slice_in_dim(everyone, here // heads * seq, seq + 2 * length)
+    meta = meta_rows(seg_ext.astype(f32), length)
     grad_attn = lax.dot_general(out_weight, out_grad, NT, preferred_element_type=f32)
     g = swap(grad_attn.reshape(heads, -1, length))
     channels = g.shape[1]
-    head = lax.rem(lax.axis_index("ctx"), heads)
-    taps = lax.dynamic_slice_in_dim(conv_weight.astype(f32).T, head * FD, FD, 0)
+    taps = lax.dynamic_slice_in_dim(conv_weight.astype(f32).T, lax.rem(here, heads) * FD, FD, 0)
     taps = jnp.pad(taps, ((0, 0), (0, 128 - taps.shape[1])))
-    edge_before = onward(pk[-1, :V_ROW])
-    edge_after = back(pk[0, :V_ROW])
-    meta = meta_rows(pk, edge_before, edge_after)
-    ext, nf = channels + FD, (FD // 2 + 2) * FD
-    seq = heads * length
-    (ending,) = call(ending_kernel, (pk, meta), [(ext, nf)], flops=4 * ext * nf * seq)
-    part, du, inc, pay = call(
+    ext, nf, chunks = channels + FD, (FD // 2 + 2) * FD, heads // BLOCKS
+    work = ext * nf * seq
+    (ending,) = call(ending_kernel, (pk, meta), [(ext + FD, nf)], 4 * work)
+    u, gext, states, inc, pay = call(
         forward_kernel,
-        (pk, g, meta, taps, edge_before[:FD], onward(ending)),
-        [(heads, ext, length), (FD, seq), (heads // BLOCKS, ext, nf), (ext + FD, nf)],
-        [(FD, seq)],
-        flops=40 * ext * nf * seq,
+        (pk, g, meta, taps, onward(ending)),
+        [(FD, seq), (ext, seq), (chunks, ext, nf), (chunks, ext, nf), (ext + FD, nf)],
+        20 * work,
+    )
+    pay = back(pay)
+    part, du = call(
+        inner_kernel, (pk, meta, u, gext, states), [(heads, ext, length), (FD, seq)], 20 * work
     )
     (out,) = call(
         backward_kernel,
-        (pk, meta, taps, part, du, inc, back(pay)),
+        (pk, meta, taps, part, du, inc, pay),
         [(heads, ext + FD, length)],
-        flops=10 * ext * nf * seq,
+        10 * work,
     )
     out = swap(out)
     return (

time: 103 us -> 129 us (1.25)
  blocking collectives: 22.9 us -> 71.2 us
  waiting for transfers between devices: 22 us -> 8.47 us
  starting transfers between devices: 22.3 us -> 12.6 us
  Pallas kernels: 15.8 us -> 18.1 us
    all_gather x0 -> x1, blocking collectives: none -> 48.5 us  [by_heads(): lax.all_gather(seg_ids, 'ctx', tiled=True) + 1]
    ppermute x2 -> x1, waiting for transfers between devices: 10.3 us -> 1.64 us  [by_heads(): lax.ppermute(x, 'ctx', [(h + heads, h) for h in range(heads)])]
    ppermute x2 -> x1, starting transfers between devices: 9.78 us -> 1.3 us  [by_heads(): lax.ppermute(x, 'ctx', [(h, h + heads) for h in range(heads)])]
    ppermute x2 -> x1, waiting for transfers between devices: 8.18 us -> 3.99 us  [by_heads(): lax.ppermute(x, 'ctx', [(h, h + heads) for h in range(heads)])]
    pallas_call x3 -> x4, Pallas kernels: 15.8 us -> 18.1 us  [call(): pl.pallas_call(kernel, out_shape=shapes, in_specs=[pl.BlockSpec(memory_sp...]
    convert_element_type x6 -> x2, other arithmetic: 2.25 us -> 0.17 us  [the longest x1 0.09 us: by_heads(): meta = meta_rows(seg_ext.astype(f32), length)]
    another operation x1 -> x2, other arithmetic: 0.65 us -> 2.02 us  [meta_rows(): return jnp.pad(jnp.stack(rows), ((0, 6), (0, 0)))]
    ppermute x2 -> x1, starting transfers between devices: 2.58 us -> 1.32 us  [by_heads(): lax.ppermute(x, 'ctx', [(h + heads, h) for h in range(heads)])]
  transfers between devices with their start and end apart: 6 -> 4, of which waited for: 4 -> 3; matrix products, arithmetic and copies ran while one was open for 13% -> 10% of each run, Pallas kernels for 2% -> 6%
where the time goes in v3:
time: 129 us
  blocking collectives  71.2 us (55%)
  Pallas kernels  18.1 us (14%)
  starting transfers between devices  12.6 us (10%)
  matrix products  9.1 us (7%)
  waiting for transfers between devices  8.47 us (7%)
  local copies, waits for them, and re-layouts  4.6 us (4%)
  other arithmetic  3.98 us (3%)
    all_gather x1, blocking collectives, by_heads(): lax.all_gather(seg_ids, 'ctx', tiled=True) + 1  48.5 us
    all_to_all x1, blocking collectives, by_heads(): swap = lambda x: lax.all_to_all(x, 'ctx', 0, 0, axis_index_groups=groups)  22.7 us
    pallas_call x4, Pallas kernels, call(): pl.pallas_call(kernel, out_shape=shapes, in_specs=[pl.BlockSpec(memory_sp...  18.1 us
    all_to_all x2, starting transfers between devices, by_heads(): swap = lambda x: lax.all_to_all(x, 'ctx', 0, 0, axis_index_groups=groups)  9.94 us
    dot_general x1, matrix products, by_heads(): lax.dot_general(out_weight, out_grad, NT, preferred_element_type=f32)  9.1 us
    ppermute x1, waiting for transfers between devices, by_heads(): lax.ppermute(x, 'ctx', [(h, h + heads) for h in range(heads)])  3.99 us
    all_to_all x2, waiting for transfers between devices, by_heads(): swap = lambda x: lax.all_to_all(x, 'ctx', 0, 0, axis_index_groups=groups)  2.84 us
  transfers between devices with their start and end apart: 4, of which 3 were waited for; matrix products, arithmetic and copies ran while one was open for 10% of the time, Pallas kernels for 6%

profile of v3, /device:TPU:0, one launch (start us, length us, event | category | flops | bytes accessed | tf_op | source)
XLA Modules:
  0.0 128.7 jit_solution(1927578836139288703)
XLA Ops:
  0.6 0.0 copy-start
  0.6 1.4 %copy.13 = bf16[2048,128]{1,0:T(8,128)(2,1)S(1)} copy(bf16[2048,128]{0,1:T(8,128)(2,1)} %bitcast.34) | data formatting | bytes 1048576 | tf_op jit(solution)/shard_map/transpose | solution.py:397
  2.0 1.8 %pad_maximum_fusion = bf16[16,160,128]{2,1,0:T(8,128)(2,1)} fusion(bf16[16,128,128]{2,1,0:T(8,128)(2,1)S(1)} %bitcast.31, bf16[16,16,128]{2,1,0:T(8,128)(2,1)} %bitcast.37, bf16[16,16,128]{2,1,0:T(8,128)(2,1)} %bitcast.38), kind=kLoop, calls=%fused_computation | loop fusion | flops 1966080 | bytes 1310720 | tf_op jit(solution)/shard_map/concatenate | solution.py:397
  3.8 6.3 %all-to-all-start = ((bf16[16,160,128]{2,1,0:T(8,128)(2,1)}), bf16[16,160,128]{2,1,0:T(8,128)(2,1)S(1)}, u32[]{:S(2)}, u32[]{:S(2)}) async-start(bf16[16,160,128]{2,1,0:T(8,128)(2,1)} %pad_maximum_fusion), calls=%async_computation | async-start | bytes 1310720 | tf_op jit(solution)/shard_map/all_to_all | solution.py:403
  10.1 0.0 copy-done
  10.1 9.1 %fusion.7 = f32[2048,128]{1,0:T(8,128)} fusion(bf16[2048,4096]{1,0:T(8,128)(2,1)} %param.12, bf16[128,4096]{1,0:T(8,128)(2,1)S(1)} %copy-done), kind=kOutput, calls=%fused_computation.21 | convolution fusion | flops 2147483648 | bytes 18874368 | tf_op jit(solution)/shard_map/dot_general | solution.py:412
  19.2 0.0 copy-start.2
  19.2 2.8 %all-to-all-done.pk_ref = bf16[16,160,128]{2,1,0:T(8,128)(2,1)S(1)} async-done(((bf16[16,160,128]{2,1,0:T(8,128)(2,1)}), bf16[16,160,128]{2,1,0:T(8,128)(2,1)S(1)}, u32[]{:S(2)}, u32[]{:S(2)}) %all-to-all-start) | async-done | bytes 655392 | tf_op jit(solution)/shard_map/all_to_all | solution.py:403
  22.1 3.7 %all-to-all-start.1 = ((f32[16,128,128]{2,1,0:T(8,128)}), f32[16,128,128]{2,1,0:T(8,128)S(1)}, u32[]{:S(2)}, u32[]{:S(2)}) async-start(f32[16,128,128]{2,1,0:T(8,128)} %bitcast.32), calls=%async_computation.1 | async-start | bytes 2097152 | tf_op jit(solution)/shard_map/all_to_all | solution.py:403
  25.7 0.0 copy-start.1
  25.8 0.0 copy-done.2
  25.8 48.5 %all-gather = s32[32,1,128]{2,1,0:T(1,128)S(1)} all-gather(s32[1,1,128]{2,1,0:T(1,128)S(1)} %bitcast.53), channel_id=1, replica_groups=mesh['ctx'=32,'head'=1] {'ctx'}, dimensions={0}, use_global_device_ids=true | all-gather | bytes 16896 | tf_op jit(solution)/shard_map/all_gather | solution.py:409
  74.3 0.1 fusion
  74.4 0.1 slice.52
  74.5 0.1 broadcast_in_dim.6
  74.6 0.1 broadcast_bitcast_fusion
  74.6 0.6 fusion.6
  75.2 0.7 compare_convert_fusion
  75.9 1.4 %compare_convert_fusion.1 = (f32[2048]{0:T(1024)S(1)}, f32[2048]{0:T(1024)S(1)}, f32[2048]{0:T(1024)S(1)}, f32[2048]{0:T(1024)S(1)}, f32[2048]{0:T(1024)S(1)}, /...) fusion(f32[]{:T(128)} %bitcast.15, f32[2304]{0:T(1024)S(1)} %fusion, f32[1792]{0:T(1024)S(1)} %slice.54, ...), kind=kLoop, calls=%fused_computation.13 | loop fusion | flops 32768 | bytes 121864 | tf_op jit(solution)/shard_map/stack | solution.py:391
  77.3 0.1 stack.79
  77.4 1.7 %shard_map.94 = f32[160,160]{1,0:T(8,128)S(1)} custom-call(bf16[16,160,128]{2,1,0:T(8,128)(2,1)S(1)} %all-to-all-done.pk_ref, f32[16,2048]{1,0:T(8,128)S(1)} %pad.14.meta_ref), custom_call_target="tpu_custom_call" | custom-call | flops 188743680 | bytes 2097152 | tf_op jit(solution)/shard_map/pallas_call | solution.py:369
  79.1 1.3 %collective-permute-start = (f32[160,160]{1,0:T(8,128)S(1)}, f32[160,160]{1,0:T(8,128)S(1)}, u32[]{:S(2)}, u32[]{:S(2)}) collective-permute-start(f32[160,160]{1,0:T(8,128)S(1)} %shard_map.94), channel_id=1, source_target_pairs={{0,16},{1,17},{2,18},{3,19},{4,20},{5,21},{6,22},{7,23},{8,24},{9,... | collective-permute-start | bytes 307208 | tf_op jit(solution)/shard_map/ppermute | solution.py:404
  80.4 0.0 copy-done.1
  80.5 0.1 dynamic-slice_convert_fusion
  80.5 0.1 copy.16
  80.6 4.0 %collective-permute-done.state_ref = f32[160,160]{1,0:T(8,128)S(1)} collective-permute-done((f32[160,160]{1,0:T(8,128)S(1)}, f32[160,160]{1,0:T(8,128)S(1)}, u32[]{:S(2)}, u32[]{:S(2)}) %collective-permute-start) | collective-permute-done | bytes 102432 | tf_op jit(solution)/shard_map/ppermute | solution.py:404
  84.6 0.0 all-to-all-done.1.g_ref
  84.6 7.8 %shard_map.95 = (f32[16,2048]{1,0:T(8,128)S(1)}, f32[144,2048]{1,0:T(8,128)S(1)}, f32[8,144,160]{2,1,0:T(8,128)S(1)}, f32[8,144,160]{2,1,0:T(8,128)S(1)}, f32[160,160]{1,0:T(8,128)S(1)}) custom-call(bf16[16,160,128]{2,1,0:T(8,128)(2,1)S(1)} %all-to-all-done.pk_ref, f32[16,128,128]{2,1,0:T(8,128)S(1)} %all-to-all-done.1.g_ref, f32[16,2048]{1,0:T(8,128)S(1)} %pad.14.meta_ref, ...), custom_call_target="tpu_custom_call" | custom-call | flops 943718400 | bytes 2097152 | tf_op jit(solution)/shard_map/pallas_call | solution.py:369
  92.4 1.3 %collective-permute-start.1 = (f32[160,160]{1,0:T(8,128)S(1)}, f32[160,160]{1,0:T(8,128)S(1)}, u32[]{:S(2)}, u32[]{:S(2)}) collective-permute-start(f32[160,160]{1,0:T(8,128)S(1)} %get-tuple-element.16), channel_id=1, source_target_pairs={{16,0},{17,1},{18,2},{19,3},{20,4},{21,5},{22,6},{23,7},{24,8},{25... | collective-permute-start | bytes 307208 | tf_op jit(solution)/shard_map/ppermute | solution.py:405
  93.8 5.9 %shard_map.96 = (f32[16,144,128]{2,1,0:T(8,128)S(1)}, f32[16,2048]{1,0:T(8,128)S(1)}) custom-call(bf16[16,160,128]{2,1,0:T(8,128)(2,1)S(1)} %all-to-all-done.pk_ref, f32[16,2048]{1,0:T(8,128)S(1)} %pad.14.meta_ref, f32[16,2048]{1,0:T(8,128)S(1)} %get-tuple-element.10.u_ref, f32[144,2048]{1,0:T(8,128)S(1)} %get-tuple-element.11.gext_ref, ...), custom_call_target="tpu_custom_call" | custom-call | flops 943718400 | bytes 2097152 | tf_op jit(solution)/shard_map/pallas_call | solution.py:369
  99.7 1.6 %collective-permute-done.1.pay_ref = f32[160,160]{1,0:T(8,128)S(1)} collective-permute-done((f32[160,160]{1,0:T(8,128)S(1)}, f32[160,160]{1,0:T(8,128)S(1)}, u32[]{:S(2)}, u32[]{:S(2)}) %collective-permute-start.1) | collective-permute-done | bytes 102432 | tf_op jit(solution)/shard_map/ppermute | solution.py:405
  101.3 2.6 %shard_map.97 = f32[16,160,128]{2,1,0:T(8,128)S(1)} custom-call(bf16[16,160,128]{2,1,0:T(8,128)(2,1)S(1)} %all-to-all-done.pk_ref, f32[16,2048]{1,0:T(8,128)S(1)} %pad.14.meta_ref, f32[16,128]{1,0:T(8,128)S(1)} %pad.15.taps_ref, f32[16,144,128]{2,1,0:T(8,128)S(1)} %get-tuple-element.13.part_ref, f32[16,2048]{1,0:T(8,128)S(1)} %get-tuple-element.14.du_ref, ...), custom_call_target="tpu_custom_call" | custom-call | flops 471859200 | bytes 2097152 | tf_op jit(solution)/shard_map/pallas_call | solution.py:369
  104.0 22.7 %all_to_all.15 = f32[16,160,128]{2,1,0:T(8,128)S(1)} all-to-all(f32[16,160,128]{2,1,0:T(8,128)S(1)} %shard_map.97), channel_id=1, replica_groups={{0,1,2,3,4,5,6,7,8,9,10,11,12,13,14,15},{16,17,18,19,20,21,22,23,24,25,..., dimensions={0} | all-to-all | bytes 2621440 | tf_op jit(solution)/shard_map/all_to_all | solution.py:403
  126.6 0.1 slice.65
  126.7 1.3 %copy.15 = f32[2048,128]{0,1:T(8,128)} copy(f32[2048,128]{1,0:T(8,128)S(1)} %bitcast.30) | data formatting | bytes 2097152 | tf_op jit(solution)/shard_map/reshape | solution.py:440
  128.0 0.7 fusion.5
  (6 shorter events, 0.1 us)
Async XLA Ops:
  0.6 9.5 %copy-start = (bf16[128,4096]{1,0:T(8,128)(2,1)S(1)}, bf16[128,4096]{1,0:T(8,128)(2,1)}, u32[]{:S(2)}) copy-start(bf16[128,4096]{1,0:T(8,128)(2,1)} %param.13) | copy-start | bytes 3145732
  3.8 18.2 %all-to-all-start = ((bf16[16,160,128]{2,1,0:T(8,128)(2,1)}), bf16[16,160,128]{2,1,0:T(8,128)(2,1)S(1)}, u32[]{:S(2)}, u32[]{:S(2)}) async-start(bf16[16,160,128]{2,1,0:T(8,128)(2,1)} %pad_maximum_fusion), calls=%async_computation | async-start | bytes 1310720 | tf_op jit(solution)/shard_map/all_to_all | solution.py:403
  19.2 6.5 %copy-start.2 = (s32[128]{0:T(128)S(1)}, s32[128]{0:T(128)}, u32[]{:S(2)}) copy-start(s32[128]{0:T(128)} %param.10) | copy-start | bytes 1540
  22.1 62.6 %all-to-all-start.1 = ((f32[16,128,128]{2,1,0:T(8,128)}), f32[16,128,128]{2,1,0:T(8,128)S(1)}, u32[]{:S(2)}, u32[]{:S(2)}) async-start(f32[16,128,128]{2,1,0:T(8,128)} %bitcast.32), calls=%async_computation.1 | async-start | bytes 2097152 | tf_op jit(solution)/shard_map/all_to_all | solution.py:403
  25.7 54.7 %copy-start.1 = (bf16[3,256]{1,0:T(4,128)(2,1)S(1)}, bf16[3,256]{1,0:T(4,128)(2,1)}, u32[]{:S(2)}) copy-start(bf16[3,256]{1,0:T(4,128)(2,1)} %param.11) | copy-start | bytes 4612
  79.1 5.5 %collective-permute-start = (f32[160,160]{1,0:T(8,128)S(1)}, f32[160,160]{1,0:T(8,128)S(1)}, u32[]{:S(2)}, u32[]{:S(2)}) collective-permute-start(f32[160,160]{1,0:T(8,128)S(1)} %shard_map.94), channel_id=1, source_target_pairs={{0,16},{1,17},{2,18},{3,19},{4,20},{5,21},{6,22},{7,23},{8,24},{9,... | collective-permute-start | bytes 307208 | tf_op jit(solution)/shard_map/ppermute | solution.py:404
  92.4 8.9 %collective-permute-start.1 = (f32[160,160]{1,0:T(8,128)S(1)}, f32[160,160]{1,0:T(8,128)S(1)}, u32[]{:S(2)}, u32[]{:S(2)}) collective-permute-start(f32[160,160]{1,0:T(8,128)S(1)} %get-tuple-element.16), channel_id=1, source_target_pairs={{16,0},{17,1},{18,2},{19,3},{20,4},{21,5},{22,6},{23,7},{24,8},{25... | collective-permute-start | bytes 307208 | tf_op jit(solution)/shard_map/ppermute | solution.py:405

commit v4 on v3

--- a/solution.py
+++ b/solution.py
@@ -160,7 +160,8 @@
 NT = (((1,), (1,)), ((), ()))
 TN = (((0,), (0,)), ((), ()))
 BLOCKS = 2
-V_ROW = 2 * FD
+SEG_ROW = 2 * FD
+V_ROW = 3 * FD
 
 
 def split(x):
@@ -230,7 +231,7 @@
     size = BLOCKS * pk_ref.shape[2]
 
     def step(i, state):
-        tail = meta_ref[8:9, lanes(i, size)]
+        tail = meta_ref[0:1, lanes(i, size)]
         feat_k = split(phi(key_rows(pk_ref, i).astype(f32)) * tail)
         vext = value_rows(pk_ref, i)
         return state + dot(vext, feat_k[0], NT) + dot(vext, feat_k[1], NT)
@@ -391,10 +392,11 @@
     return jnp.pad(jnp.stack(rows), ((0, 6), (0, 0)))
 
 
-def pack(queries, keys, values):
+def pack(queries, keys, values, seg_ids):
     heads, length = queries.shape[0] // FD, queries.shape[1]
     shaped = lambda x: x.reshape(heads, -1, length)
-    return jnp.concatenate([shaped(queries), shaped(keys), shaped(values.T)], axis=1)
+    seg = jnp.broadcast_to((seg_ids + 1).astype(bf16), (heads, FD, length))
+    return jnp.concatenate([shaped(queries), shaped(keys), seg, shaped(values.T)], axis=1)
 
 
 def by_heads(queries, keys, values, seg_ids, conv_weight, out_weight, out_grad):
@@ -405,9 +407,12 @@
     back = lambda x: lax.ppermute(x, "ctx", [(h + heads, h) for h in range(heads)])
     here = lax.axis_index("ctx")
     seq = heads * length
-    pk = swap(pack(queries, keys, values))
-    everyone = jnp.pad(lax.all_gather(seg_ids, "ctx", tiled=True) + 1, (length, length))
-    seg_ext = lax.dynamic_slice_in_dim(everyone, here // heads * seq, seq + 2 * length)
+    pk = swap(pack(queries, keys, values, seg_ids))
+    edge_before = onward(pk[-1, SEG_ROW:V_ROW])[0]
+    edge_after = back(pk[0, SEG_ROW:V_ROW])[0]
+    seg = pk[:, SEG_ROW].reshape(-1)
+    open_end = jnp.broadcast_to((seg == seg[-1]).astype(f32), (FD, seq))
+    seg_ext = jnp.concatenate([edge_before, seg, edge_after])
     meta = meta_rows(seg_ext.astype(f32), length)
     grad_attn = lax.dot_general(out_weight, out_grad, NT, preferred_element_type=f32)
     g = swap(grad_attn.reshape(heads, -1, length))
@@ -416,7 +421,7 @@
     taps = jnp.pad(taps, ((0, 0), (0, 128 - taps.shape[1])))
     ext, nf, chunks = channels + FD, (FD // 2 + 2) * FD, heads // BLOCKS
     work = ext * nf * seq
-    (ending,) = call(ending_kernel, (pk, meta), [(ext + FD, nf)], 4 * work)
+    (ending,) = call(ending_kernel, (pk, open_end), [(ext + FD, nf)], 4 * work)
     u, gext, states, inc, pay = call(
         forward_kernel,
         (pk, g, meta, taps, onward(ending)),

time: 129 us -> 94.9 us (0.74)
  blocking collectives: 71.2 us -> 28 us
  starting transfers between devices: 12.6 us -> 22.5 us
  waiting for transfers between devices: 8.47 us -> 6 us
  between operations: 0.78 us -> 2.15 us
    all_gather x1 -> x0, blocking collectives: 48.5 us -> none  [by_heads(): lax.all_gather(seg_ids, 'ctx', tiled=True) + 1]
    ppermute x1 -> x2, starting transfers between devices: 1.3 us -> 9.94 us  [by_heads(): lax.ppermute(x, 'ctx', [(h, h + heads) for h in range(heads)])]
    all_to_all x1, blocking collectives: 22.7 us -> 28 us  [by_heads(): swap = lambda x: lax.all_to_all(x, 'ctx', 0, 0, axis_index_groups=groups)]
    ppermute x1 -> x2, waiting for transfers between devices: 3.99 us -> 1.54 us  [by_heads(): lax.ppermute(x, 'ctx', [(h, h + heads) for h in range(heads)])]
    another operation x2, other arithmetic: 2.02 us -> 0.09 us  [meta_rows(): return jnp.pad(jnp.stack(rows), ((0, 6), (0, 0)))]
    convert_element_type x0 -> x2, other arithmetic: none -> 1.4 us  [the longest x1 0.75 us: pack(): seg = jnp.broadcast_to((seg_ids + 1).astype(bf16), (heads, FD, length))]
    ppermute x1 -> x2, starting transfers between devices: 1.32 us -> 2.61 us  [by_heads(): lax.ppermute(x, 'ctx', [(h + heads, h) for h in range(heads)])]
  transfers between devices with their start and end apart: 4 -> 6, of which waited for: 3 -> 3; matrix products, arithmetic and copies ran while one was open for 10% -> 12% of each run, Pallas kernels for 6% -> 8%
where the time goes in v4:
time: 94.9 us; the launch traced here: 94.4 us
  blocking collectives  28 us (30%)
  starting transfers between devices  22.5 us (24%)
  Pallas kernels  18.1 us (19%)
  matrix products  9.1 us (10%)
  waiting for transfers between devices  6 us (6%)
  local copies, waits for them, and re-layouts  5.15 us (5%)
  other arithmetic  3.37 us (4%)
  between operations  2.15 us (2%)
    all_to_all x1, blocking collectives, by_heads(): swap = lambda x: lax.all_to_all(x, 'ctx', 0, 0, axis_index_groups=groups)  28 us
    pallas_call x4, Pallas kernels, call(): pl.pallas_call(kernel, out_shape=shapes, in_specs=[pl.BlockSpec(memory_sp...  18.1 us
    all_to_all x2, starting transfers between devices, by_heads(): swap = lambda x: lax.all_to_all(x, 'ctx', 0, 0, axis_index_groups=groups)  9.94 us
    ppermute x2, starting transfers between devices, by_heads(): lax.ppermute(x, 'ctx', [(h, h + heads) for h in range(heads)])  9.94 us
    dot_general x1, matrix products, by_heads(): lax.dot_general(out_weight, out_grad, NT, preferred_element_type=f32)  9.1 us
    all_to_all x2, waiting for transfers between devices, by_heads(): swap = lambda x: lax.all_to_all(x, 'ctx', 0, 0, axis_index_groups=groups)  3.54 us
    ppermute x2, starting transfers between devices, by_heads(): lax.ppermute(x, 'ctx', [(h + heads, h) for h in range(heads)])  2.61 us
  transfers between devices with their start and end apart: 6, of which 3 were waited for; matrix products, arithmetic and copies ran while one was open for 12% of the time, Pallas kernels for 8%

profile of v4, /device:TPU:0, one launch (start us, length us, event | category | flops | bytes accessed | tf_op | source)
XLA Modules:
  0.0 94.4 jit_solution(2118955793977504143)
XLA Ops:
  0.6 0.0 copy-start
  0.6 0.7 add_convert_fusion
  1.4 1.3 %copy.13 = bf16[2048,128]{1,0:T(8,128)(2,1)S(1)} copy(bf16[2048,128]{0,1:T(8,128)(2,1)} %bitcast.45) | data formatting | bytes 1048576 | tf_op jit(solution)/shard_map/transpose | solution.py:399
  2.7 1.8 %pad_maximum_fusion = bf16[16,176,128]{2,1,0:T(8,128)(2,1)} fusion(bf16[16,128,128]{2,1,0:T(8,128)(2,1)S(1)} %bitcast.42, bf16[16,16,128]{2,1,0:T(8,128)(2,1)S(1)} %broadcast_in_dim.12, bf16[16,16,128]{2,1,0:T(8,128)(2,1)} %bitcast.48, bf16[16,16,128]{2,1,0:T(8,128)(2,1)} %bitcast.49), kind=kLoop, calls=%fused_computation | loop fusion | flops 2883584 | bytes 1441792 | tf_op jit(solution)/shard_map/concatenate | solution.py:399
  4.5 6.3 %all-to-all-start = ((bf16[16,176,128]{2,1,0:T(8,128)(2,1)}), bf16[16,176,128]{2,1,0:T(8,128)(2,1)S(1)}, u32[]{:S(2)}, u32[]{:S(2)}) async-start(bf16[16,176,128]{2,1,0:T(8,128)(2,1)} %pad_maximum_fusion), calls=%async_computation | async-start | bytes 1441792 | tf_op jit(solution)/shard_map/all_to_all | solution.py:405
  10.8 0.0 copy-done
  10.8 9.1 %fusion.5 = f32[2048,128]{1,0:T(8,128)} fusion(bf16[2048,4096]{1,0:T(8,128)(2,1)} %param.12, bf16[128,4096]{1,0:T(8,128)(2,1)S(1)} %copy-done), kind=kOutput, calls=%fused_computation.25 | convolution fusion | flops 2147483648 | bytes 18874368 | tf_op jit(solution)/shard_map/dot_general | solution.py:417
  19.9 0.0 copy-start.1
  19.9 3.5 %all-to-all-done.pk_ref = bf16[16,176,128]{2,1,0:T(8,128)(2,1)S(1)} async-done(((bf16[16,176,128]{2,1,0:T(8,128)(2,1)}), bf16[16,176,128]{2,1,0:T(8,128)(2,1)S(1)}, u32[]{:S(2)}, u32[]{:S(2)}) %all-to-all-start) | async-done | bytes 720928 | tf_op jit(solution)/shard_map/all_to_all | solution.py:405
  23.5 3.7 %all-to-all-start.1 = ((f32[16,128,128]{2,1,0:T(8,128)}), f32[16,128,128]{2,1,0:T(8,128)S(1)}, u32[]{:S(2)}, u32[]{:S(2)}) async-start(f32[16,128,128]{2,1,0:T(8,128)} %bitcast.43), calls=%async_computation.1 | async-start | bytes 2097152 | tf_op jit(solution)/shard_map/all_to_all | solution.py:405
  27.1 0.0 copy-done.1
  27.2 0.1 dynamic-slice_convert_fusion
  27.2 0.1 copy.16
  27.4 0.6 slice.110
  28.6 4.5 %collective-permute-start = (bf16[16,128]{1,0:T(8,128)(2,1)S(1)}, bf16[16,128]{1,0:T(8,128)(2,1)S(1)}, u32[]{:S(2)}, u32[]{:S(2)}) collective-permute-start(bf16[16,128]{1,0:T(8,128)(2,1)S(1)} %get-tuple-element.19), channel_id=1, source_target_pairs={{0,16},{1,17},{2,18},{3,19},{4,20},{5,21},{6,22},{7,23},{8,24},{9,... | collective-permute-start | bytes 12296 | tf_op jit(solution)/shard_map/ppermute | solution.py:406
  33.1 1.3 %collective-permute-start.1 = (bf16[16,128]{1,0:T(8,128)(2,1)S(1)}, bf16[16,128]{1,0:T(8,128)(2,1)S(1)}, u32[]{:S(2)}, u32[]{:S(2)}) collective-permute-start(bf16[16,128]{1,0:T(8,128)(2,1)S(1)} %get-tuple-element.20), channel_id=1, source_target_pairs={{16,0},{17,1},{18,2},{19,3},{20,4},{21,5},{22,6},{23,7},{24,8},{25... | collective-permute-start | bytes 12296 | tf_op jit(solution)/shard_map/ppermute | solution.py:407
  34.4 0.7 compare_convert_fusion
  35.1 1.7 %shard_map.94 = f32[160,160]{1,0:T(8,128)S(1)} custom-call(bf16[16,176,128]{2,1,0:T(8,128)(2,1)S(1)} %all-to-all-done.pk_ref, f32[16,2048]{1,0:T(8,128)S(1)} %broadcast_in_dim.15.meta_ref), custom_call_target="tpu_custom_call" | custom-call | flops 188743680 | bytes 2097152 | tf_op jit(solution)/shard_map/pallas_call | solution.py:370
  36.8 5.5 %collective-permute-start.2 = (f32[160,160]{1,0:T(8,128)S(1)}, f32[160,160]{1,0:T(8,128)S(1)}, u32[]{:S(2)}, u32[]{:S(2)}) collective-permute-start(f32[160,160]{1,0:T(8,128)S(1)} %shard_map.94), channel_id=1, source_target_pairs={{0,16},{1,17},{2,18},{3,19},{4,20},{5,21},{6,22},{7,23},{8,24},{9,... | collective-permute-start | bytes 307208 | tf_op jit(solution)/shard_map/ppermute | solution.py:406
  42.3 0.0 collective-permute-done
  42.3 0.6 slice.106
  43.5 0.0 collective-permute-done.1
  43.6 0.1 slice.75
  43.7 0.1 broadcast_in_dim.13
  43.8 0.1 broadcast_bitcast_fusion
  43.8 0.1 compare_convert_fusion.2
  43.9 0.1 stack.79
  44.1 1.5 %collective-permute-done.2.state_ref = f32[160,160]{1,0:T(8,128)S(1)} collective-permute-done((f32[160,160]{1,0:T(8,128)S(1)}, f32[160,160]{1,0:T(8,128)S(1)}, u32[]{:S(2)}, u32[]{:S(2)}) %collective-permute-start.2) | collective-permute-done | bytes 102432 | tf_op jit(solution)/shard_map/ppermute | solution.py:406
  45.6 0.0 all-to-all-done.1.g_ref
  45.6 7.8 %shard_map.95 = (f32[16,2048]{1,0:T(8,128)S(1)}, f32[144,2048]{1,0:T(8,128)S(1)}, f32[8,144,160]{2,1,0:T(8,128)S(1)}, f32[8,144,160]{2,1,0:T(8,128)S(1)}, f32[160,160]{1,0:T(8,128)S(1)}) custom-call(bf16[16,176,128]{2,1,0:T(8,128)(2,1)S(1)} %all-to-all-done.pk_ref, f32[16,128,128]{2,1,0:T(8,128)S(1)} %all-to-all-done.1.g_ref, f32[16,2048]{1,0:T(8,128)S(1)} %pad.9.meta_ref, ...), custom_call_target="tpu_custom_call" | custom-call | flops 943718400 | bytes 2097152 | tf_op jit(solution)/shard_map/pallas_call | solution.py:370
  53.5 1.3 %collective-permute-start.3 = (f32[160,160]{1,0:T(8,128)S(1)}, f32[160,160]{1,0:T(8,128)S(1)}, u32[]{:S(2)}, u32[]{:S(2)}) collective-permute-start(f32[160,160]{1,0:T(8,128)S(1)} %get-tuple-element.16), channel_id=1, source_target_pairs={{16,0},{17,1},{18,2},{19,3},{20,4},{21,5},{22,6},{23,7},{24,8},{25... | collective-permute-start | bytes 307208 | tf_op jit(solution)/shard_map/ppermute | solution.py:407
  54.8 5.9 %shard_map.96 = (f32[16,144,128]{2,1,0:T(8,128)S(1)}, f32[16,2048]{1,0:T(8,128)S(1)}) custom-call(bf16[16,176,128]{2,1,0:T(8,128)(2,1)S(1)} %all-to-all-done.pk_ref, f32[16,2048]{1,0:T(8,128)S(1)} %pad.9.meta_ref, f32[16,2048]{1,0:T(8,128)S(1)} %get-tuple-element.10.u_ref, f32[144,2048]{1,0:T(8,128)S(1)} %get-tuple-element.11.gext_ref, ...), custom_call_target="tpu_custom_call" | custom-call | flops 943718400 | bytes 2097152 | tf_op jit(solution)/shard_map/pallas_call | solution.py:370
  60.7 0.9 collective-permute-done.3.pay_ref
  61.6 2.6 %shard_map.97 = f32[16,160,128]{2,1,0:T(8,128)S(1)} custom-call(bf16[16,176,128]{2,1,0:T(8,128)(2,1)S(1)} %all-to-all-done.pk_ref, f32[16,2048]{1,0:T(8,128)S(1)} %pad.9.meta_ref, f32[16,128]{1,0:T(8,128)S(1)} %pad.10.taps_ref, f32[16,144,128]{2,1,0:T(8,128)S(1)} %get-tuple-element.13.part_ref, f32[16,2048]{1,0:T(8,128)S(1)} %get-tuple-element.14.du_ref, ...), custom_call_target="tpu_custom_call" | custom-call | flops 471859200 | bytes 2097152 | tf_op jit(solution)/shard_map/pallas_call | solution.py:370
  64.2 28.0 %all_to_all.15 = f32[16,160,128]{2,1,0:T(8,128)S(1)} all-to-all(f32[16,160,128]{2,1,0:T(8,128)S(1)} %shard_map.97), channel_id=1, replica_groups={{0,1,2,3,4,5,6,7,8,9,10,11,12,13,14,15},{16,17,18,19,20,21,22,23,24,25,..., dimensions={0} | all-to-all | bytes 2621440 | tf_op jit(solution)/shard_map/all_to_all | solution.py:405
  92.3 0.1 slice.93
  92.4 1.3 %copy.15 = f32[2048,128]{0,1:T(8,128)} copy(f32[2048,128]{1,0:T(8,128)S(1)} %bitcast.41) | data formatting | bytes 2097152 | tf_op jit(solution)/shard_map/reshape | solution.py:445
  93.7 0.7 fusion.4
  (13 shorter events, 0.1 us)
Async XLA Ops:
  0.6 10.2 %copy-start = (bf16[128,4096]{1,0:T(8,128)(2,1)S(1)}, bf16[128,4096]{1,0:T(8,128)(2,1)}, u32[]{:S(2)}) copy-start(bf16[128,4096]{1,0:T(8,128)(2,1)} %param.13) | copy-start | bytes 3145732
  4.5 18.9 %all-to-all-start = ((bf16[16,176,128]{2,1,0:T(8,128)(2,1)}), bf16[16,176,128]{2,1,0:T(8,128)(2,1)S(1)}, u32[]{:S(2)}, u32[]{:S(2)}) async-start(bf16[16,176,128]{2,1,0:T(8,128)(2,1)} %pad_maximum_fusion), calls=%async_computation | async-start | bytes 1441792 | tf_op jit(solution)/shard_map/all_to_all | solution.py:405
  19.9 7.2 %copy-start.1 = (bf16[3,256]{1,0:T(4,128)(2,1)S(1)}, bf16[3,256]{1,0:T(4,128)(2,1)}, u32[]{:S(2)}) copy-start(bf16[3,256]{1,0:T(4,128)(2,1)} %param.11) | copy-start | bytes 4612
  23.5 22.2 %all-to-all-start.1 = ((f32[16,128,128]{2,1,0:T(8,128)}), f32[16,128,128]{2,1,0:T(8,128)S(1)}, u32[]{:S(2)}, u32[]{:S(2)}) async-start(f32[16,128,128]{2,1,0:T(8,128)} %bitcast.43), calls=%async_computation.1 | async-start | bytes 2097152 | tf_op jit(solution)/shard_map/all_to_all | solution.py:405
  28.6 13.7 %collective-permute-start = (bf16[16,128]{1,0:T(8,128)(2,1)S(1)}, bf16[16,128]{1,0:T(8,128)(2,1)S(1)}, u32[]{:S(2)}, u32[]{:S(2)}) collective-permute-start(bf16[16,128]{1,0:T(8,128)(2,1)S(1)} %get-tuple-element.19), channel_id=1, source_target_pairs={{0,16},{1,17},{2,18},{3,19},{4,20},{5,21},{6,22},{7,23},{8,24},{9,... | collective-permute-start | bytes 12296 | tf_op jit(solution)/shard_map/ppermute | solution.py:406
  33.1 10.4 %collective-permute-start.1 = (bf16[16,128]{1,0:T(8,128)(2,1)S(1)}, bf16[16,128]{1,0:T(8,128)(2,1)S(1)}, u32[]{:S(2)}, u32[]{:S(2)}) collective-permute-start(bf16[16,128]{1,0:T(8,128)(2,1)S(1)} %get-tuple-element.20), channel_id=1, source_target_pairs={{16,0},{17,1},{18,2},{19,3},{20,4},{21,5},{22,6},{23,7},{24,8},{25... | collective-permute-start | bytes 12296 | tf_op jit(solution)/shard_map/ppermute | solution.py:407
  36.8 8.8 %collective-permute-start.2 = (f32[160,160]{1,0:T(8,128)S(1)}, f32[160,160]{1,0:T(8,128)S(1)}, u32[]{:S(2)}, u32[]{:S(2)}) collective-permute-start(f32[160,160]{1,0:T(8,128)S(1)} %shard_map.94), channel_id=1, source_target_pairs={{0,16},{1,17},{2,18},{3,19},{4,20},{5,21},{6,22},{7,23},{8,24},{9,... | collective-permute-start | bytes 307208 | tf_op jit(solution)/shard_map/ppermute | solution.py:406
  53.5 8.1 %collective-permute-start.3 = (f32[160,160]{1,0:T(8,128)S(1)}, f32[160,160]{1,0:T(8,128)S(1)}, u32[]{:S(2)}, u32[]{:S(2)}) collective-permute-start(f32[160,160]{1,0:T(8,128)S(1)} %get-tuple-element.16), channel_id=1, source_target_pairs={{16,0},{17,1},{18,2},{19,3},{20,4},{21,5},{22,6},{23,7},{24,8},{25... | collective-permute-start | bytes 307208 | tf_op jit(solution)/shard_map/ppermute | solution.py:407
